TPU v7x, 256 devices: a whole 4x4x8 slice. The times are simulated.
256 devices in a mesh: dp: 4 (over y_hi, core), seq: 64 (over z, y_lo, x).
Axes of the slice: x: 4, y: 4 (y_hi: 2, y_lo: 2; y = y_hi * 2 + y_lo), z: 8, core: 2. Of those that a mesh axis runs over, the one named last changes fastest.
Arguments:
- space_query: bfloat16 [256, 704, 576], P(('dp', 'seq')), parts along dimension 0, may hold values from -8 to 8
- space_key: bfloat16 [256, 704, 576], P(('dp', 'seq')), parts along dimension 0, may hold values from -8 to 8
- space_value: bfloat16 [256, 704, 576], P(('dp', 'seq')), parts along dimension 0, may hold values from -6 to 6
- space_output: bfloat16 [256, 704, 576], P(('dp', 'seq')), parts along dimension 0, may hold values from -6 to 6
- space_upstream: bfloat16 [256, 704, 576], P(('dp', 'seq')), parts along dimension 0, may hold values from -6 to 6
- time_query: bfloat16 [256, 704, 576], P(('dp', 'seq')), parts along dimension 0, may hold values from -8 to 8
- time_key: bfloat16 [256, 704, 576], P(('dp', 'seq')), parts along dimension 0, may hold values from -8 to 8
- time_value: bfloat16 [256, 704, 576], P(('dp', 'seq')), parts along dimension 0, may hold values from -6 to 6
- time_output: bfloat16 [256, 704, 576], P(('dp', 'seq')), parts along dimension 0, may hold values from -6 to 6
- time_upstream: bfloat16 [256, 704, 576], P(('dp', 'seq')), parts along dimension 0, may hold values from -6 to 6
Outputs:
- space_query_grad: bfloat16 [256, 704, 576], P(('dp', 'seq')), parts along dimension 0
- space_key_grad: bfloat16 [256, 704, 576], P(('dp', 'seq')), parts along dimension 0
- space_value_grad: bfloat16 [256, 704, 576], P(('dp', 'seq')), parts along dimension 0
- time_query_grad: bfloat16 [256, 704, 576], P(('dp', 'seq')), parts along dimension 0
- time_key_grad: bfloat16 [256, 704, 576], P(('dp', 'seq')), parts along dimension 0
- time_value_grad: bfloat16 [256, 704, 576], P(('dp', 'seq')), parts along dimension 0
There are 4 independent parts, one for each index of `dp`. A program takes and returns all parts, laid end to end along the dimension named above; each array names one. Nothing has to cross between parts.
All inputs are finite; a program needn't handle non-finite values.
Results may differ from a plain program's by a relative error of at most 0.0054.
Values may be sent and summed in bfloat16 or wider, within the bound.
No kernel may reach another device: no remote copies, remote signals or barrier semaphores. Data moves between devices by JAX's collectives and lax.ppermute only.
A program may use at most 64 MiB of HBM per device.

v0:
```python
import math

import jax
import jax.numpy as jnp
from jax import lax
from jax.experimental import pallas as pl
from jax.experimental.pallas import tpu as pltpu
from jax.sharding import PartitionSpec as P

HEADS = 8
DIM = 72
WIDTH = HEADS * DIM
TOKENS = 704
FRAMES = 64
BULK = 512
EXTRA = TOKENS - BULK
SEND = 200
BACK = 152
UNITS = 22
ROWS = 4 * FRAMES
TILE = DIM // 8
SCALE = 1.0 / math.sqrt(DIM)
EXP_SCALE = SCALE * math.log2(math.e)
VMEM = 50 * 1024 * 1024
BF16 = jnp.bfloat16
F32 = jnp.float32
NN = ((1,), (0,))
NT = ((1,), (1,))
TN = ((0,), (0,))


def dot(a, b, dims):
    return lax.dot_general(a, b, (dims, ((), ())), preferred_element_type=F32)


def iota(shape, axis):
    return lax.broadcasted_iota(jnp.int32, shape, axis)


def ones_where(condition):
    return jnp.where(condition, 1.0, 0.0).astype(BF16)


def roll(x, shift):
    return pltpu.roll(x, shift, x.ndim - 1)


def pack_kernel(*refs):
    main, extra, out_ref = refs[:5], refs[5:10], refs[10]
    b = pl.program_id(0)
    q, k, v, g, o = [ref[...].astype(F32) for ref in main]
    left = iota((WIDTH, 128), 1) < 64
    row = iota((EXTRA, 256), 0)
    lane = iota((EXTRA, 256), 1)
    base = 24 * (2 * b + lane // 128)
    spread = None
    for c in range(4):
        at = lane % 128 - 24 * c
        pick = ones_where((at >= 0) & (at < 24) & (row == base + at))
        part = dot(extra[c][:, :EXTRA], pick, NN)
        spread = part if spread is None else spread + part
    dots_main = jnp.sum((g * o).reshape(HEADS, DIM, 128), axis=1)
    more = extra[3][:, :EXTRA].astype(F32) * extra[4][:, :EXTRA].astype(F32)
    dots_more = jnp.sum(more.reshape(HEADS, DIM, EXTRA), axis=1)
    tail = None
    for dots, size in ((dots_main, 128), (dots_more, EXTRA)):
        shape = (HEADS, 8, size)
        kept = jnp.where(iota(shape, 2) % 4 == iota(shape, 1) % 4, dots[:, None, :], 0.0)
        token = iota((size, 256), 0)
        lane = iota((size, 256), 1)
        if size == 128:
            pick = (token // 64 == lane // 128) & ((token % 64) // 4 == lane % 128 - 96)
        else:
            at = token - 24 * (2 * b + lane // 128)
            pick = (at >= 0) & (at < 24) & (at // 4 == lane % 128 - 112)
        part = dot(kept.reshape(64, size).astype(BF16), ones_where(pick), NN)
        tail = part if tail is None else tail + part
    body_lane = iota((HEADS, 7, 8, 128), 3) < 96
    for side in range(2):
        pairs = []
        for x, y in ((q, k), (v, g)):
            joined = jnp.where(left, x, roll(y, 64)) if side == 0 else jnp.where(left, roll(x, 64), y)
            pairs.append(joined.reshape(HEADS, TILE, 8, 128))
        rest = spread[:, 128 * side : 128 * side + 128].reshape(HEADS, TILE, 8, 128)
        filler = [roll(rest[:, t], 96 - 32 * p) for t in (7, 8) for p in range(3)]
        filler.append(tail[:, 128 * side : 128 * side + 128].reshape(HEADS, 8, 128))
        rest = jnp.where(body_lane, rest[:, :7], jnp.stack(filler, axis=1))
        message = jnp.concatenate([*pairs, rest], axis=1).reshape(HEADS * SEND, 128)
        out_ref[side * HEADS * SEND : (side + 1) * HEADS * SEND, :] = message.astype(BF16)


def unpack_kernel(in_ref, *out_refs):
    b = pl.program_id(0)
    size = HEADS * BACK

    def block(a):
        start = pl.multiple_of(a * size, 16)
        return in_ref[pl.ds(start, size), :].astype(F32).reshape(HEADS, BACK // 8, 8, 128)

    @pl.when(b < 4)
    def _():
        one, two = block(2 * b), block(2 * b + 1)
        left = iota((HEADS, TILE, 8, 128), 3) < 64
        first, second = one[:, :TILE], two[:, :TILE]
        grads = (
            jnp.where(left, first, roll(second, 64)),
            jnp.where(left, roll(first, 64), second),
            jnp.where(left, one[:, TILE : 2 * TILE], roll(two[:, TILE : 2 * TILE], 64)),
        )
        for ref, grad in zip(out_refs, grads):
            ref[...] = grad.reshape(WIDTH, 128).astype(BF16)

    for step, owners in ((4, range(6)), (5, range(4, 8))):

        @pl.when(b == step)
        def _(step=step, owners=owners):
            blocks = [block(a) for a in owners]
            token = 128 * (step - 4) + iota((256, 128), 1)
            row = iota((256, 128), 0)
            sums = [None] * 3
            for i in range(0, len(blocks), 2):
                wide = [x[:, TILE : 2 * TILE].reshape(WIDTH, 128) for x in blocks[i : i + 2]]
                wide = jnp.concatenate(wide, axis=1).astype(BF16)
                at = token - 24 * (owners[i] + row // 128)
                for c in range(3):
                    inside = (at >= 0) & (at < (24, 24, 16)[c])
                    pick = ones_where(inside & (row % 128 == 64 + 24 * c + at))
                    part = dot(wide, pick, NN)
                    sums[c] = part if sums[c] is None else sums[c] + part
            left_over = jnp.stack([x[:, 2 * TILE] for x in blocks], axis=1)
            left_over = left_over.reshape(HEADS, 8 * len(blocks), 128).astype(BF16)
            shape = (8 * len(blocks), 128)
            row = iota(shape, 0)
            place = 24 * (owners[0] + row // 8) + 16 + row % 8
            pick = ones_where(128 * (step - 4) + iota(shape, 1) == place)
            last = [dot(left_over[h], pick, TN)[:DIM] for h in range(HEADS)]
            sums[2] = sums[2] + jnp.concatenate(last, axis=0)
            for ref, grad in zip(out_refs, sums):
                ref[...] = grad.astype(BF16)


def softmax_t(scores):
    top = jnp.max(scores, axis=0, keepdims=True)
    weights = jnp.exp2((scores - top) * EXP_SCALE)
    return weights * (1.0 / jnp.sum(weights, axis=0, keepdims=True))


def time_kernel(in_ref, out_ref, held, tails, grads):
    row = iota((256, 256), 0)
    order = ones_where(iota((256, 256), 1) == 128 * ((row // 4) % 2) + 4 * (row // 8) + row % 4)
    lane = iota((8, 128), 1)
    upper = iota((8, 128), 0) < 4

    def arrive(i, carry):
        start = pl.multiple_of(i * 2 * SEND, 16)
        at = pl.ds(pl.multiple_of(i * 8, 8), 8)
        x = in_ref[pl.ds(start, 2 * SEND), :].astype(F32).reshape(2, SEND // 8, 8, 128)
        rests = []
        for f in range(2):
            m = x[f, 2 * TILE :]
            ends = [
                jnp.where(
                    lane < 32,
                    roll(m[t], 32),
                    jnp.where(lane < 64, roll(m[t + 1], 64), roll(m[t + 2], 96)),
                )
                for t in (0, 3)
            ]
            rests.append(jnp.concatenate([m, ends[0][None], ends[1][None]], axis=0))
        sets = (
            (x[0, :TILE], x[1, :TILE]),
            (x[0, TILE : 2 * TILE], x[1, TILE : 2 * TILE]),
            rests,
        )
        turned = []
        for parts in sets:
            wide = jnp.concatenate([p.reshape(DIM, 128) for p in parts], axis=1).astype(BF16)
            turned.append(dot(order, wide, NT).reshape(32, 8, DIM))
        for c in range(4):
            half = turned[c // 2]
            held[c, 0:16, at, 0:DIM] = half[16 * (c % 2) : 16 * (c % 2) + 16]
            held[c, 16:UNITS, at, 0:DIM] = turned[2][6 * c : 6 * c + 6]
        tails[at, :] = jnp.where(upper, x[0, SEND // 8 - 1], x[1, SEND // 8 - 1])
        return carry

    lax.fori_loop(0, FRAMES // 2, arrive, 0, unroll=16)
    pick = ones_where(iota((32, 128), 1) == iota((32, 128), 0) + 96)
    dots = dot(pick, tails[...].astype(BF16), NT)
    same = iota((ROWS, ROWS), 0) % 4 == iota((ROWS, ROWS), 1) % 4
    for u in range(UNITS):
        q, k, v, g = [held[c, u, :, 0:DIM].astype(BF16) for c in range(4)]
        attend = softmax_t(jnp.where(same, dot(k, q, NT), -1e30))
        dscore = (attend * (dot(v, g, NT) - dots[u : u + 1, :])).astype(BF16)
        grads[0, u, :, 0:DIM] = dot(dscore, k, TN) * SCALE
        grads[1, u, :, 0:DIM] = dot(dscore, q, NN) * SCALE
        grads[2, u, :, 0:DIM] = dot(attend.astype(BF16), g, NN)

    def leave(i, carry):
        at = pl.ds(pl.multiple_of(i * 8, 8), 8)
        sets = (
            (grads[0, 0:16, at, 0:DIM], grads[1, 0:16, at, 0:DIM]),
            (
                grads[2, 0:16, at, 0:DIM],
                grads[0, 16:UNITS, at, 0:DIM],
                grads[1, 16:UNITS, at, 0:DIM],
                grads[2, 16:20, at, 0:DIM],
            ),
        )
        turned = []
        for parts in sets:
            rows = jnp.concatenate(parts, axis=0).reshape(256, DIM).astype(BF16)
            turned.append(dot(rows, order, TN))
        a = jnp.where(lane < DIM, grads[2, 20, at, :], 0.0)
        c = jnp.where(lane < DIM, grads[2, 21, at, :], 0.0)
        ends = (
            jnp.where(upper, a, pltpu.roll(c, 4, 0)),
            jnp.where(upper, pltpu.roll(a, 4, 0), c),
        )
        pieces = []
        for f in range(2):
            pieces += [t[:, 128 * f : 128 * f + 128] for t in turned] + [ends[f]]
        start = pl.multiple_of(i * 2 * BACK, 16)
        out_ref[pl.ds(start, 2 * BACK), :] = jnp.concatenate(pieces, axis=0).astype(BF16)
        return carry

    lax.fori_loop(0, FRAMES // 2, leave, 0, unroll=16)


def space_kernel(q_ref, k_ref, v_ref, o_ref, g_ref, dq_ref, dk_ref, dv_ref):
    q2, k2, v2, o2, g2 = [ref[...].astype(F32) for ref in (q_ref, k_ref, v_ref, o_ref, g_ref)]
    dots = jnp.sum((g2 * o2).reshape(2, DIM, TOKENS), axis=1)
    grads = ([], [], [])
    for h in range(2):
        part = slice(h * DIM, (h + 1) * DIM)
        q, k, v, g = [x[part].astype(BF16) for x in (q2, k2, v2, g2)]
        k_rows, v_rows = k2[part].T.astype(BF16), v2[part].T.astype(BF16)
        dq, dk, dv = [], None, None
        for start, size in ((0, 256), (256, 256), (512, 192)):
            cols = slice(start, start + size)
            attend = softmax_t(dot(k_rows, q[:, cols], NN))
            shifted = dot(v_rows, g[:, cols], NN) - dots[h : h + 1, cols]
            dscore = (attend * shifted).astype(BF16)
            dq.append(dot(k, dscore, NN))
            dk_part = dot(q[:, cols], dscore, NT)
            dv_part = dot(g[:, cols], attend.astype(BF16), NT)
            dk = dk_part if dk is None else dk + dk_part
            dv = dv_part if dv is None else dv + dv_part
        grads[0].append(jnp.concatenate(dq, axis=1) * SCALE)
        grads[1].append(dk * SCALE)
        grads[2].append(dv)
    for ref, halves in zip((dq_ref, dk_ref, dv_ref), grads):
        ref[...] = jnp.concatenate(halves, axis=0).astype(BF16)


def call(kernel, out_shapes, args, flops, **specs):
    moved = sum(a.size * 2 for a in args) + sum(math.prod(o) * 2 for o in out_shapes)
    return pl.pallas_call(
        kernel,
        out_shape=tuple(jax.ShapeDtypeStruct(o, BF16) for o in out_shapes),
        compiler_params=pltpu.CompilerParams(vmem_limit_bytes=VMEM),
        cost_estimate=pl.CostEstimate(flops=flops, bytes_accessed=moved, transcendentals=0),
        name=kernel.__name__,
        **specs,
    )(*args)


def pack(q, k, v, g, o):
    main = pl.BlockSpec((WIDTH, 128), lambda b: (0, b))
    extra = pl.BlockSpec((WIDTH, 256), lambda b: (0, 2))
    return call(
        pack_kernel,
        [(FRAMES * SEND, 128)],
        (q, k, v, g, o) * 2,
        10**9,
        grid=(4,),
        in_specs=[main] * 5 + [extra] * 5,
        out_specs=(pl.BlockSpec((16 * SEND, 128), lambda b: (b, 0)),),
    )[0]


def unpack(back):
    return call(
        unpack_kernel,
        [(WIDTH, TOKENS)] * 3,
        (back,),
        10**9,
        grid=(6,),
        in_specs=[pl.BlockSpec((FRAMES * BACK, 128), lambda b: (0, 0))],
        out_specs=(pl.BlockSpec((WIDTH, 128), lambda b: (0, b)),) * 3,
    )


def time_grads(got):
    return call(
        time_kernel,
        [(FRAMES * BACK, 128)],
        (got,),
        10**10,
        scratch_shapes=[
            pltpu.VMEM((4, UNITS, ROWS, 128), F32),
            pltpu.VMEM((ROWS, 128), F32),
            pltpu.VMEM((3, UNITS, ROWS, 128), F32),
        ],
    )[0]


def space_grads(*args):
    spec = pl.BlockSpec((2 * DIM, TOKENS), lambda b: (b, 0))
    return call(
        space_kernel,
        [(WIDTH, TOKENS)] * 3,
        args,
        4 * 10**10,
        grid=(4,),
        in_specs=[spec] * 5,
        out_specs=(spec,) * 3,
    )


def exchange(x, rows):
    x = x.reshape(FRAMES, rows, 128)
    x = lax.all_to_all(x, "seq", split_axis=0, concat_axis=0, tiled=True)
    return x.reshape(FRAMES * rows, 128)


def body(*args):
    sq, sk, sv, so, sg, tq, tk, tv, to, tg = [jnp.swapaxes(x[0], 0, 1) for x in args]
    got = exchange(pack(tq, tk, tv, tg, to), SEND)
    space = space_grads(sq, sk, sv, so, sg)
    time = unpack(exchange(time_grads(got), BACK))
    return tuple(jnp.swapaxes(x, 0, 1)[None] for x in (*space, *time))


def solution(mesh):
    spec = P(("dp", "seq"), None, None)
    return jax.shard_map(
        body, mesh=mesh, in_specs=(spec,) * 10, out_specs=(spec,) * 6, check_vma=False
    )
```

profile of v0, /device:TPU:2, one launch (start us, length us, event | category | flops | bytes accessed | tf_op | source)
XLA Modules:
  0.0 186.7 jit_solution(4753053880023920981)
XLA Ops:
  0.6 0.0 copy-start
  0.6 1.2 copy-done
  1.8 0.0 copy-start.1
  1.8 1.2 copy-done.1
  3.0 0.0 copy-start.2
  3.0 1.2 copy-done.2
  4.1 0.0 copy-start.3
  4.1 1.2 copy-done.3
  5.3 6.0 %pack_kernel.1 = bf16[12800,128]{1,0:T(8,128)(2,1)} custom-call(bf16[576,704]{1,0:T(8,128)(2,1)S(1)} %bitcast.52, bf16[576,704]{1,0:T(8,128)(2,1)S(1)} %bitcast.54, bf16[576,704]{1,0:T(8,128)(2,1)S(1)} %bitcast.56, bf16[576,704]{1,0:T(8,128)(2,1)S(1)} %bitcast.58, bf16[576,704]{1,0:T(8,128)(2,1)} %bitcast.67, bf16[576,704]{1,0:T(8,128)(2,1)S(1)} %bitcast.53, ...), custom_call_target="tpu_custom_call" | custom-call | flops 1000000000 | bytes 11386880 | tf_op jit(solution)/shard_map/pack_kernel/pallas_call | solution.py:257
  11.3 88.8 %all_to_all.10 = bf16[64,200,128]{2,1,0:T(8,128)(2,1)} all-to-all(bf16[64,200,128]{2,1,0:T(8,128)(2,1)} %bitcast.66), channel_id=1, replica_groups=mesh['dp'=4,'seq'=64] {'seq'}, dimensions={0} | all-to-all | bytes 6553600 | tf_op jit(solution)/shard_map/all_to_all | solution.py:322
  100.1 15.7 %time_kernel.1 = bf16[9728,128]{1,0:T(8,128)(2,1)S(1)} custom-call(bf16[12800,128]{1,0:T(8,128)(2,1)} %bitcast.69), custom_call_target="tpu_custom_call" | custom-call | flops 10000000000 | bytes 5767168 | tf_op jit(solution)/shard_map/time_kernel/pallas_call | solution.py:257
  115.8 0.0 copy-start.4
  115.9 1.5 copy-done.4
  117.3 0.0 copy-start.5
  117.3 7.0 %all-to-all-start.1 = ((bf16[64,152,128]{2,1,0:T(8,128)(2,1)}), bf16[64,152,128]{2,1,0:T(8,128)(2,1)S(1)}, u32[]{:S(2)}, u32[]{:S(2)}) async-start(bf16[64,152,128]{2,1,0:T(8,128)(2,1)} %bitcast.61), calls=%async_computation.1 | async-start | bytes 4980736 | tf_op jit(solution)/shard_map/all_to_all | solution.py:322
  124.3 0.0 copy-done.5
  124.3 0.0 copy-start.6
  124.3 1.2 copy-done.6
  125.5 0.0 copy-start.7
  125.5 1.2 copy-done.7
  126.7 0.0 copy-start.8
  126.7 1.2 copy-done.8
  127.8 19.7 %space_kernel.1 = (bf16[576,704]{1,0:T(8,128)(2,1)}, bf16[576,704]{1,0:T(8,128)(2,1)}, bf16[576,704]{1,0:T(8,128)(2,1)}) custom-call(bf16[576,704]{1,0:T(8,128)(2,1)S(1)} %bitcast.62, bf16[576,704]{1,0:T(8,128)(2,1)S(1)} %bitcast.63, bf16[576,704]{1,0:T(8,128)(2,1)S(1)} %bitcast.64, bf16[576,704]{1,0:T(8,128)(2,1)S(1)} %bitcast.65, bf16[576,704]{1,0:T(8,128)(2,1)} %bitcast.70), custom_call_target="tpu_custom_call" | custom-call | flops 40000000000 | bytes 6488064 | tf_op jit(solution)/shard_map/space_kernel/pallas_call | solution.py:257
  147.6 34.7 %all-to-all-done.1 = bf16[64,152,128]{2,1,0:T(8,128)(2,1)S(1)} async-done(((bf16[64,152,128]{2,1,0:T(8,128)(2,1)}), bf16[64,152,128]{2,1,0:T(8,128)(2,1)S(1)}, u32[]{:S(2)}, u32[]{:S(2)}) %all-to-all-start.1) | async-done | bytes 2490400 | tf_op jit(solution)/shard_map/all_to_all | solution.py:322
  182.2 4.5 %unpack_kernel.1 = (bf16[576,704]{1,0:T(8,128)(2,1)}, bf16[576,704]{1,0:T(8,128)(2,1)}, bf16[576,704]{1,0:T(8,128)(2,1)}) custom-call(bf16[9728,128]{1,0:T(8,128)(2,1)S(1)} %bitcast.60), custom_call_target="tpu_custom_call" | custom-call | flops 1000000000 | bytes 4923392 | tf_op jit(solution)/shard_map/unpack_kernel/pallas_call | solution.py:257
Async XLA Ops:
  0.6 1.2 copy-start
  1.8 1.2 copy-start.1
  3.0 1.2 copy-start.2
  4.1 1.2 copy-start.3
  115.8 1.5 copy-start.4
  117.3 7.0 %copy-start.5 = (bf16[1,704,576]{1,2,0:T(8,128)(2,1)S(1)}, bf16[1,704,576]{1,2,0:T(8,128)(2,1)}, u32[]{:S(2)}) copy-start(bf16[1,704,576]{1,2,0:T(8,128)(2,1)} %param.10) | copy-start | bytes 2433028
  117.3 64.9 %all-to-all-start.1 = ((bf16[64,152,128]{2,1,0:T(8,128)(2,1)}), bf16[64,152,128]{2,1,0:T(8,128)(2,1)S(1)}, u32[]{:S(2)}, u32[]{:S(2)}) async-start(bf16[64,152,128]{2,1,0:T(8,128)(2,1)} %bitcast.61), calls=%async_computation.1 | async-start | bytes 4980736 | tf_op jit(solution)/shard_map/all_to_all | solution.py:322
  124.3 1.2 copy-start.6
  125.5 1.2 copy-start.7
  126.7 1.2 copy-start.8
where the time goes:
time: 187 us
  blocking collectives  88.8 us (47%)
  Pallas kernels  46 us (25%)
  waiting for transfers between devices  34.7 us (19%)
  local copies, waits for them, and re-layouts  9.62 us (5%)
  starting transfers between devices  6.99 us (4%)
    all_to_all x1, blocking collectives, exchange(): x = lax.all_to_all(x, 'seq', split_axis=0, concat_axis=0, tiled=True)  88.8 us
    pallas_call x4, Pallas kernels, call(): pl.pallas_call(kernel, out_shape=tuple((jax.ShapeDtypeStruct(o, BF16) for...  46 us
    all_to_all x1, waiting for transfers between devices, exchange(): x = lax.all_to_all(x, 'seq', split_axis=0, concat_axis=0, tiled=True)  34.7 us
    unnamed x18, local copies, waits for them, and re-layouts  9.62 us
    all_to_all x1, starting transfers between devices, exchange(): x = lax.all_to_all(x, 'seq', split_axis=0, concat_axis=0, tiled=True)  6.99 us
  transfers between devices with their start and end apart: 1, of which 1 were waited for; matrix products, arithmetic and copies ran while one was open for 0% of the time, Pallas kernels for 11%

commit v1 on v0

v1 whole, which is shorter than its diff:
```python
import math

import jax
import jax.numpy as jnp
from jax import lax
from jax.experimental import pallas as pl
from jax.experimental.pallas import tpu as pltpu
from jax.sharding import PartitionSpec as P

HEADS = 8
DIM = 72
WIDTH = HEADS * DIM
TOKENS = 704
FRAMES = 64
BULK = 512
EXTRA = TOKENS - BULK
SEND = 200
BACK = 152
UNITS = 22
ROWS = 4 * FRAMES
TILE = DIM // 8
SCALE = 1.0 / math.sqrt(DIM)
EXP_SCALE = SCALE * math.log2(math.e)
BF16 = jnp.bfloat16
F32 = jnp.float32
NN = ((1,), (0,))
NT = ((1,), (1,))
TN = ((0,), (0,))


def dot(a, b, dims):
    return lax.dot_general(a, b, (dims, ((), ())), preferred_element_type=F32)


def iota(shape, axis):
    return lax.broadcasted_iota(jnp.int32, shape, axis)


def ones_where(condition):
    return jnp.where(condition, 1.0, 0.0).astype(BF16)


def roll(x, shift):
    return pltpu.roll(x, shift, x.ndim - 1)


def pack_kernel(q_ref, k_ref, v_ref, g_ref, o_ref, out_ref, picks, dot_pick):
    @pl.when(pl.program_id(0) == 0)
    def _():
        shape = (EXTRA, 128)
        row, lane = iota(shape, 0), iota(shape, 1)
        for a in range(8):
            at = row - 24 * a
            mine = (at >= 0) & (at < 24)
            cols = slice(128 * a, 128 * a + 128)
            for c in range(4):
                picks[c, :, cols] = ones_where(mine & (lane == at + 24 * c))
            dot_pick[:, cols] = ones_where(mine & (lane == 112 + at // 4))

    refs = (q_ref, k_ref, v_ref, g_ref)
    q, k, v, g = [ref[:, :BULK].astype(F32) for ref in refs]
    spread = None
    for c in range(4):
        part = dot(refs[c][:, BULK:], picks[c], NN)
        spread = part if spread is None else spread + part
    prod = g_ref[...].astype(F32) * o_ref[...].astype(F32)
    dots = jnp.sum(prod.reshape(2, DIM, TOKENS), axis=1)
    shape = (2, 8, TOKENS)
    kept = jnp.where(iota(shape, 2) % 4 == iota(shape, 1) % 4, dots[:, None, :], 0.0)
    kept = kept.reshape(16, TOKENS).astype(BF16)
    token, lane = iota((128, 256), 0), iota((128, 256), 1)
    pick = (token // 64 == lane // 128) & ((token % 64) // 4 == lane % 128 - 96)
    stacked = jnp.concatenate([kept[:, 128 * b : 128 * b + 128] for b in range(4)], axis=0)
    tail = dot(stacked, ones_where(pick), NN)
    tail_more = dot(kept[:, BULK:], dot_pick[...], NN)
    left = iota((2 * DIM, 128), 1) < 64
    body_lane = iota((2, 7, 8, 128), 3) < 96
    for a in range(8):
        b, odd = a // 2, a % 2
        cols = slice(128 * b, 128 * b + 128)
        pairs = []
        for x, y in ((q[:, cols], k[:, cols]), (v[:, cols], g[:, cols])):
            joined = jnp.where(left, roll(x, 64), y) if odd else jnp.where(left, x, roll(y, 64))
            pairs.append(joined.reshape(2, TILE, 8, 128))
        cols = slice(128 * a, 128 * a + 128)
        rest = spread[:, cols].reshape(2, TILE, 8, 128)
        filler = [roll(rest[:, t], 96 - 32 * p) for t in (7, 8) for p in range(3)]
        here = tail[16 * b : 16 * b + 16, 128 * odd : 128 * odd + 128] + tail_more[:, cols]
        filler.append(here.reshape(2, 8, 128))
        rest = jnp.where(body_lane, rest[:, :7], jnp.stack(filler, axis=1))
        message = jnp.concatenate([*pairs, rest], axis=1).reshape(2 * SEND, 128)
        out_ref[a] = message.astype(BF16)


def unpack_kernel(in_ref, dq_ref, dk_ref, dv_ref, picks, end_pick):
    @pl.when(pl.program_id(0) == 0)
    def _():
        shape = (128, EXTRA)
        row, token = iota(shape, 0), iota(shape, 1)
        for a in range(8):
            at = token - 24 * a
            for c in range(3):
                mine = (at >= 0) & (at < (24, 24, 16)[c]) & (row == 64 + 24 * c + at)
                rows = slice(128 * (a % 2), 128 * (a % 2) + 128)
                picks[a // 2, rows, 256 * c : 256 * c + EXTRA] = ones_where(mine)
                picks[a // 2, rows, 256 * c + EXTRA : 256 * c + 256] = jnp.zeros((128, 64), BF16)
        shape = (64, EXTRA)
        row = iota(shape, 0)
        end_pick[...] = ones_where(iota(shape, 1) == 24 * (row // 8) + 16 + row % 8)

    left = iota((2, TILE, 8, 128), 3) < 64
    more, ends = None, []
    for b in range(4):
        one, two = [
            in_ref[a].astype(F32).reshape(2, BACK // 8, 8, 128) for a in (2 * b, 2 * b + 1)
        ]
        cols = slice(128 * b, 128 * b + 128)
        first, second = one[:, :TILE], two[:, :TILE]
        third, fourth = one[:, TILE : 2 * TILE], two[:, TILE : 2 * TILE]
        grads = (
            jnp.where(left, first, roll(second, 64)),
            jnp.where(left, roll(first, 64), second),
            jnp.where(left, third, roll(fourth, 64)),
        )
        for ref, grad in zip((dq_ref, dk_ref, dv_ref), grads):
            ref[:, cols] = grad.reshape(2 * DIM, 128).astype(BF16)
        wide = jnp.concatenate([x.reshape(2 * DIM, 128) for x in (third, fourth)], axis=1)
        part = dot(wide.astype(BF16), picks[b], NN)
        more = part if more is None else more + part
        ends += [one[:, 2 * TILE], two[:, 2 * TILE]]
    ends = jnp.stack(ends, axis=1).reshape(2, 64, 128).astype(BF16)
    last = [dot(ends[h], end_pick[...], TN)[:DIM] for h in range(2)]
    for c, ref in enumerate((dq_ref, dk_ref, dv_ref)):
        grad = more[:, 256 * c : 256 * c + EXTRA]
        if c == 2:
            grad = grad + jnp.concatenate(last, axis=0)
        ref[:, BULK:] = grad.astype(BF16)


def softmax_t(scores):
    top = jnp.max(scores, axis=0, keepdims=True)
    weights = jnp.exp2((scores - top) * EXP_SCALE)
    return weights * (1.0 / jnp.sum(weights, axis=0, keepdims=True))


def time_kernel(in_ref, out_ref, held, tails, grads):
    row = iota((256, 256), 0)
    order = ones_where(iota((256, 256), 1) == 128 * ((row // 4) % 2) + 4 * (row // 8) + row % 4)
    lane = iota((8, 128), 1)
    upper = iota((8, 128), 0) < 4

    def arriving(i):
        start = pl.multiple_of(i * 2 * SEND, 16)
        x = in_ref[pl.ds(start, 2 * SEND), :].astype(F32).reshape(2, SEND // 8, 8, 128)
        rests = []
        for f in range(2):
            m = x[f, 2 * TILE :]
            ends = [
                jnp.where(
                    lane < 32,
                    roll(m[t], 32),
                    jnp.where(lane < 64, roll(m[t + 1], 64), roll(m[t + 2], 96)),
                )
                for t in (0, 3)
            ]
            rests.append(jnp.concatenate([m, ends[0][None], ends[1][None]], axis=0))
        sets = (
            (x[0, :TILE], x[1, :TILE]),
            (x[0, TILE : 2 * TILE], x[1, TILE : 2 * TILE]),
            rests,
        )
        turned = []
        for parts in sets:
            wide = jnp.concatenate([p.reshape(DIM, 128) for p in parts], axis=1).astype(BF16)
            turned.append(dot(order, wide, NT).reshape(32, 8, DIM))
        return turned, jnp.where(upper, x[0, SEND // 8 - 1], x[1, SEND // 8 - 1])

    def keep(i, turned, tail):
        at = pl.ds(pl.multiple_of(i * 8, 8), 8)
        for c in range(4):
            half = turned[c // 2]
            held[c, 0:16, at, 0:DIM] = half[16 * (c % 2) : 16 * (c % 2) + 16]
            held[c, 16:UNITS, at, 0:DIM] = turned[2][6 * c : 6 * c + 6]
        tails[at, :] = tail

    ahead(FRAMES // 2, arriving, keep)
    pick = ones_where(iota((32, 128), 1) == iota((32, 128), 0) + 96)
    dots = dot(pick, tails[...].astype(BF16), NT)
    same = iota((ROWS, ROWS), 0) % 4 == iota((ROWS, ROWS), 1) % 4

    def load(u):
        q, k, v, g = [held[c, u, :, 0:DIM].astype(BF16) for c in range(4)]
        return q, k, g, dot(k, q, NT), dot(v, g, NT)

    following = load(0)
    for u in range(UNITS):
        q, k, g, scores, grad_attend = following
        if u + 1 < UNITS:
            following = load(u + 1)
        attend = softmax_t(jnp.where(same, scores, -1e30))
        dscore = (attend * (grad_attend - dots[u : u + 1, :])).astype(BF16)
        grads[0, u, :, 0:DIM] = dot(dscore, k, TN) * SCALE
        grads[1, u, :, 0:DIM] = dot(dscore, q, NN) * SCALE
        grads[2, u, :, 0:DIM] = dot(attend.astype(BF16), g, NN)

    def leaving(i):
        at = pl.ds(pl.multiple_of(i * 8, 8), 8)
        sets = (
            (grads[0, 0:16, at, 0:DIM], grads[1, 0:16, at, 0:DIM]),
            (
                grads[2, 0:16, at, 0:DIM],
                grads[0, 16:UNITS, at, 0:DIM],
                grads[1, 16:UNITS, at, 0:DIM],
                grads[2, 16:20, at, 0:DIM],
            ),
        )
        turned = []
        for parts in sets:
            rows = jnp.concatenate(parts, axis=0).reshape(256, DIM).astype(BF16)
            turned.append(dot(rows, order, TN))
        a = jnp.where(lane < DIM, grads[2, 20, at, :], 0.0)
        c = jnp.where(lane < DIM, grads[2, 21, at, :], 0.0)
        ends = (
            jnp.where(upper, a, pltpu.roll(c, 4, 0)),
            jnp.where(upper, pltpu.roll(a, 4, 0), c),
        )
        return turned, ends

    def send(i, turned, ends):
        pieces = []
        for f in range(2):
            pieces += [t[:, 128 * f : 128 * f + 128] for t in turned] + [ends[f]]
        start = pl.multiple_of(i * 2 * BACK, 16)
        out_ref[pl.ds(start, 2 * BACK), :] = jnp.concatenate(pieces, axis=0).astype(BF16)

    ahead(FRAMES // 2, leaving, send)


def ahead(count, make, use, block=16):
    def step(j, carry):
        made = make(j * block)
        for t in range(block):
            following = make(j * block + t + 1) if t + 1 < block else None
            use(j * block + t, *made)
            made = following
        return carry

    lax.fori_loop(0, count // block, step, 0)


def space_kernel(q_ref, k_ref, v_ref, o_ref, g_ref, dq_ref, dk_ref, dv_ref):
    q2, k2, v2, o2, g2 = [ref[...].astype(F32) for ref in (q_ref, k_ref, v_ref, o_ref, g_ref)]
    dots = jnp.sum((g2 * o2).reshape(2, DIM, TOKENS), axis=1)
    grads = ([], [], [])
    for h in range(2):
        part = slice(h * DIM, (h + 1) * DIM)
        q, k, v, g = [x[part].astype(BF16) for x in (q2, k2, v2, g2)]
        k_rows, v_rows = k2[part].T.astype(BF16), v2[part].T.astype(BF16)
        dq, dk, dv = [], None, None
        for start, size in ((0, 256), (256, 256), (512, 192)):
            cols = slice(start, start + size)
            attend = softmax_t(dot(k_rows, q[:, cols], NN))
            shifted = dot(v_rows, g[:, cols], NN) - dots[h : h + 1, cols]
            dscore = (attend * shifted).astype(BF16)
            dq.append(dot(k, dscore, NN))
            dk_part = dot(q[:, cols], dscore, NT)
            dv_part = dot(g[:, cols], attend.astype(BF16), NT)
            dk = dk_part if dk is None else dk + dk_part
            dv = dv_part if dv is None else dv + dv_part
        grads[0].append(jnp.concatenate(dq, axis=1) * SCALE)
        grads[1].append(dk * SCALE)
        grads[2].append(dv)
    for ref, halves in zip((dq_ref, dk_ref, dv_ref), grads):
        ref[...] = jnp.concatenate(halves, axis=0).astype(BF16)


def call(kernel, out_shapes, args, flops, vmem, **specs):
    moved = sum(a.size * 2 for a in args) + sum(math.prod(o) * 2 for o in out_shapes)
    return pl.pallas_call(
        kernel,
        out_shape=tuple(jax.ShapeDtypeStruct(o, BF16) for o in out_shapes),
        compiler_params=pltpu.CompilerParams(vmem_limit_bytes=vmem * 1024 * 1024),
        cost_estimate=pl.CostEstimate(flops=flops, bytes_accessed=moved, transcendentals=0),
        name=kernel.__name__,
        **specs,
    )(*args)


HEAD_PAIR = pl.BlockSpec((2 * DIM, TOKENS), lambda p: (p, 0))


def pack(q, k, v, g, o):
    (sent,) = call(
        pack_kernel,
        [(8, HEADS * SEND, 128)],
        (q, k, v, g, o),
        10**9,
        60,
        grid=(4,),
        in_specs=[HEAD_PAIR] * 5,
        out_specs=(pl.BlockSpec((8, 2 * SEND, 128), lambda p: (0, p, 0)),),
        scratch_shapes=[pltpu.VMEM((4, EXTRA, 1024), BF16), pltpu.VMEM((EXTRA, 1024), BF16)],
    )
    return sent


def unpack(back):
    return call(
        unpack_kernel,
        [(WIDTH, TOKENS)] * 3,
        (back.reshape(8, HEADS * BACK, 128),),
        10**9,
        50,
        grid=(4,),
        in_specs=[pl.BlockSpec((8, 2 * BACK, 128), lambda p: (0, p, 0))],
        out_specs=(HEAD_PAIR,) * 3,
        scratch_shapes=[pltpu.VMEM((4, 256, 768), BF16), pltpu.VMEM((64, EXTRA), BF16)],
    )


def time_grads(got):
    return call(
        time_kernel,
        [(FRAMES * BACK, 128)],
        (got,),
        10**10,
        50,
        scratch_shapes=[
            pltpu.VMEM((4, UNITS, ROWS, 128), F32),
            pltpu.VMEM((ROWS, 128), F32),
            pltpu.VMEM((3, UNITS, ROWS, 128), F32),
        ],
    )[0]


def space_grads(*args):
    return call(
        space_kernel,
        [(WIDTH, TOKENS)] * 3,
        args,
        4 * 10**10,
        60,
        grid=(4,),
        in_specs=[HEAD_PAIR] * 5,
        out_specs=(HEAD_PAIR,) * 3,
    )


def exchange(x, rows):
    x = x.reshape(FRAMES, rows, 128)
    x = lax.all_to_all(x, "seq", split_axis=0, concat_axis=0, tiled=True)
    return x.reshape(FRAMES * rows, 128)


def body(*args):
    sq, sk, sv, so, sg, tq, tk, tv, to, tg = [jnp.swapaxes(x[0], 0, 1) for x in args]
    got = exchange(pack(tq, tk, tv, tg, to), SEND)
    space = space_grads(sq, sk, sv, so, sg)
    time = unpack(exchange(time_grads(got), BACK))
    return tuple(jnp.swapaxes(x, 0, 1)[None] for x in (*space, *time))


def solution(mesh):
    spec = P(("dp", "seq"), None, None)
    return jax.shard_map(
        body, mesh=mesh, in_specs=(spec,) * 10, out_specs=(spec,) * 6, check_vma=False
    )
```

time: 187 us -> 179 us (0.957)
  local copies, waits for them, and re-layouts: 9.62 us -> 1.46 us
  Pallas kernels: 46 us -> 42.7 us
  waiting for transfers between devices: 34.7 us -> 37.8 us
    unnamed x18 -> x2, local copies, waits for them, and re-layouts: 9.62 us -> 1.46 us
    pallas_call x4, Pallas kernels: 46 us -> 42.7 us  [call(): pl.pallas_call(kernel, out_shape=tuple((jax.ShapeDtypeStruct(o, BF16) for...]
    all_to_all x1, waiting for transfers between devices: 34.7 us -> 37.8 us  [exchange(): x = lax.all_to_all(x, 'seq', split_axis=0, concat_axis=0, tiled=True)]
where the time goes in v1:
time: 179 us; the launch traced here: 178 us
  blocking collectives  88.8 us (50%)
  Pallas kernels  42.7 us (24%)
  waiting for transfers between devices  37.8 us (21%)
  starting transfers between devices  6.87 us (4%)
    all_to_all x1, blocking collectives, exchange(): x = lax.all_to_all(x, 'seq', split_axis=0, concat_axis=0, tiled=True)  88.8 us
    pallas_call x4, Pallas kernels, call(): pl.pallas_call(kernel, out_shape=tuple((jax.ShapeDtypeStruct(o, BF16) for...  42.7 us
    all_to_all x1, waiting for transfers between devices, exchange(): x = lax.all_to_all(x, 'seq', split_axis=0, concat_axis=0, tiled=True)  37.8 us
    all_to_all x1, starting transfers between devices, exchange(): x = lax.all_to_all(x, 'seq', split_axis=0, concat_axis=0, tiled=True)  6.87 us
  transfers between devices with their start and end apart: 1, of which 1 were waited for; matrix products, arithmetic and copies ran while one was open for 0% of the time, Pallas kernels for 11%

profile of v1, /device:TPU:2, one launch (start us, length us, event | category | flops | bytes accessed | tf_op | source)
XLA Modules:
  0.0 178.2 jit_solution(11948763529901404112)
XLA Ops:
  0.6 6.5 %pack_kernel.1 = bf16[8,1600,128]{2,1,0:T(8,128)(2,1)} custom-call(bf16[576,704]{1,0:T(8,128)(2,1)} %bitcast.56, bf16[576,704]{1,0:T(8,128)(2,1)} %bitcast.57, bf16[576,704]{1,0:T(8,128)(2,1)} %bitcast.58, bf16[576,704]{1,0:T(8,128)(2,1)} %bitcast.59, bf16[576,704]{1,0:T(8,128)(2,1)} %bitcast.60), custom_call_target="tpu_custom_call" | custom-call | flops 1000000000 | bytes 7331840 | tf_op jit(solution)/shard_map/pack_kernel/pallas_call | solution.py:279
  7.1 88.8 %all_to_all.10 = bf16[64,200,128]{2,1,0:T(8,128)(2,1)} all-to-all(bf16[64,200,128]{2,1,0:T(8,128)(2,1)} %bitcast.54), channel_id=1, replica_groups=mesh['dp'=4,'seq'=64] {'seq'}, dimensions={0} | all-to-all | bytes 6553600 | tf_op jit(solution)/shard_map/all_to_all | solution.py:351
  95.9 12.7 %time_kernel.1 = bf16[9728,128]{1,0:T(8,128)(2,1)S(1)} custom-call(bf16[12800,128]{1,0:T(8,128)(2,1)} %bitcast.55), custom_call_target="tpu_custom_call" | custom-call | flops 10000000000 | bytes 5767168 | tf_op jit(solution)/shard_map/time_kernel/pallas_call | solution.py:279
  108.6 0.0 copy-start
  108.6 1.5 copy-done
  110.0 6.9 %all-to-all-start.1 = ((bf16[64,152,128]{2,1,0:T(8,128)(2,1)}), bf16[64,152,128]{2,1,0:T(8,128)(2,1)S(1)}, u32[]{:S(2)}, u32[]{:S(2)}) async-start(bf16[64,152,128]{2,1,0:T(8,128)(2,1)} %bitcast.53), calls=%async_computation.1 | async-start | bytes 4980736 | tf_op jit(solution)/shard_map/all_to_all | solution.py:351
  116.9 20.1 %space_kernel.1 = (bf16[576,704]{1,0:T(8,128)(2,1)}, bf16[576,704]{1,0:T(8,128)(2,1)}, bf16[576,704]{1,0:T(8,128)(2,1)}) custom-call(bf16[576,704]{1,0:T(8,128)(2,1)} %bitcast.61, bf16[576,704]{1,0:T(8,128)(2,1)} %bitcast.62, bf16[576,704]{1,0:T(8,128)(2,1)} %bitcast.63, bf16[576,704]{1,0:T(8,128)(2,1)} %bitcast.64, bf16[576,704]{1,0:T(8,128)(2,1)} %bitcast.65), custom_call_target="tpu_custom_call" | custom-call | flops 40000000000 | bytes 6488064 | tf_op jit(solution)/shard_map/space_kernel/pallas_call | solution.py:279
  137.1 37.8 %all-to-all-done.1 = bf16[64,152,128]{2,1,0:T(8,128)(2,1)S(1)} async-done(((bf16[64,152,128]{2,1,0:T(8,128)(2,1)}), bf16[64,152,128]{2,1,0:T(8,128)(2,1)S(1)}, u32[]{:S(2)}, u32[]{:S(2)}) %all-to-all-start.1) | async-done | bytes 2490400 | tf_op jit(solution)/shard_map/all_to_all | solution.py:351
  174.8 3.4 %unpack_kernel.1 = (bf16[576,704]{1,0:T(8,128)(2,1)}, bf16[576,704]{1,0:T(8,128)(2,1)}, bf16[576,704]{1,0:T(8,128)(2,1)}) custom-call(bf16[8,1216,128]{2,1,0:T(8,128)(2,1)S(1)} %bitcast.52), custom_call_target="tpu_custom_call" | custom-call | flops 1000000000 | bytes 4923392 | tf_op jit(solution)/shard_map/unpack_kernel/pallas_call | solution.py:279
Async XLA Ops:
  108.6 1.5 copy-start
  110.0 64.8 %all-to-all-start.1 = ((bf16[64,152,128]{2,1,0:T(8,128)(2,1)}), bf16[64,152,128]{2,1,0:T(8,128)(2,1)S(1)}, u32[]{:S(2)}, u32[]{:S(2)}) async-start(bf16[64,152,128]{2,1,0:T(8,128)(2,1)} %bitcast.53), calls=%async_computation.1 | async-start | bytes 4980736 | tf_op jit(solution)/shard_map/all_to_all | solution.py:351

commit v2 on v1

v2 whole, which is shorter than its diff:
```python
import math

import jax
import jax.numpy as jnp
from jax import lax
from jax.experimental import pallas as pl
from jax.experimental.pallas import tpu as pltpu
from jax.sharding import PartitionSpec as P

HEADS = 8
DIM = 72
WIDTH = HEADS * DIM
TOKENS = 704
FRAMES = 64
BULK = 512
EXTRA = TOKENS - BULK
SEND = 200
BACK = 152
UNITS = 22
ROWS = 4 * FRAMES
TILE = DIM // 8
SCALE = 1.0 / math.sqrt(DIM)
EXP_SCALE = SCALE * math.log2(math.e)
BF16 = jnp.bfloat16
F32 = jnp.float32
NN = ((1,), (0,))
NT = ((1,), (1,))
TN = ((0,), (0,))


def dot(a, b, dims):
    return lax.dot_general(a, b, (dims, ((), ())), preferred_element_type=F32)


def iota(shape, axis):
    return lax.broadcasted_iota(jnp.int32, shape, axis)


def ones_where(condition):
    return jnp.where(condition, 1.0, 0.0).astype(BF16)


def roll(x, shift):
    return pltpu.roll(x, shift, x.ndim - 1)


def turn(x, shift):
    return roll(x, shift % 128) if shift % 128 else x


def pack_kernel(q_ref, k_ref, v_ref, g_ref, o_ref, out_ref, held, made, dot_pick, in_sem, out_sem):
    refs = (q_ref, k_ref, v_ref, g_ref, o_ref)

    def fetch(c, p):
        rows = pl.ds(pl.multiple_of(p * 2 * DIM, 16), 2 * DIM)
        return pltpu.make_async_copy(refs[c].at[rows, :], held.at[c, p], in_sem.at[c, p])

    def send(p):
        rows = pl.ds(pl.multiple_of(p * 2 * SEND, 16), 2 * SEND)
        return pltpu.make_async_copy(made.at[p], out_ref.at[:, rows, :], out_sem.at[p])

    for p in range(4):
        for c in range(5):
            fetch(c, p).start()

    row, lane = iota((EXTRA, 128), 0), iota((EXTRA, 128), 1)
    for a in range(8):
        at = row - 24 * a
        mine = (at >= 0) & (at < 24) & (lane == 112 + at // 4)
        dot_pick[:, 128 * a : 128 * a + 128] = ones_where(mine)
    token, lane = iota((128, 256), 0), iota((128, 256), 1)
    pick = (token // 64 == lane // 128) & ((token % 64) // 4 == lane % 128 - 96)
    pick = ones_where(pick)
    lane = iota((2 * DIM, 128), 1)
    body_lane = iota((2, 7, 8, 128), 3) < 96
    shape = (2, 8, TOKENS)
    same = iota(shape, 2) % 4 == iota(shape, 1) % 4

    def head_pair(p, carry):
        for c in range(5):
            fetch(c, p).wait()
        full = [held[c, p].astype(F32) for c in range(4)]
        dots = jnp.sum((full[3] * held[4, p].astype(F32)).reshape(2, DIM, TOKENS), axis=1)
        kept = jnp.where(same, dots[:, None, :], 0.0).reshape(16, TOKENS).astype(BF16)
        stacked = jnp.concatenate([kept[:, 128 * b : 128 * b + 128] for b in range(4)], axis=0)
        tail = dot(stacked, pick, NN)
        tail_more = dot(kept[:, BULK:], dot_pick[...], NN)
        fourth = [x[:, BULK : BULK + 128] for x in full]
        blank = jnp.zeros((2 * DIM, 64), F32)
        fifth = [jnp.concatenate([x[:, BULK + 128 :], blank], axis=1) for x in full]
        across = [jnp.where(lane < 16, x, y) for x, y in zip(fifth, fourth)]

        def gather(a):
            b, odd = a // 2, a % 2
            cols = slice(128 * b, 128 * b + 128)
            q, k, v, g = [x[:, cols] for x in full]
            pairs = []
            for x, y in ((q, k), (v, g)):
                if odd:
                    joined = jnp.where(lane < 64, roll(x, 64), y)
                else:
                    joined = jnp.where(lane < 64, x, roll(y, 64))
                pairs.append(joined.reshape(2, TILE, 8, 128))
            source = fourth if a < 5 else across if a == 5 else fifth
            moved = [turn(x, 24 * c - 24 * a) for c, x in enumerate(source)]
            rest = moved[3]
            for c in (2, 1, 0):
                rest = jnp.where(lane < 24 * c + 24, moved[c], rest)
            return pairs, rest.reshape(2, TILE, 8, 128)

        def fold(a, pairs, rest):
            b, odd = a // 2, a % 2
            filler = [turn(rest[:, t], 96 - 32 * n) for t in (7, 8) for n in range(3)]
            here = tail[16 * b : 16 * b + 16, 128 * odd : 128 * odd + 128]
            here = here + tail_more[:, 128 * a : 128 * a + 128]
            filler.append(here.reshape(2, 8, 128))
            return pairs, rest[:, :7], jnp.stack(filler, axis=1)

        def store(a, pairs, rest, filler):
            rest = jnp.where(body_lane, rest, filler)
            message = jnp.concatenate([*pairs, rest], axis=1).reshape(2 * SEND, 128)
            made[p, a] = message.astype(BF16)

        first, second = {}, {}
        for t in range(10):
            if t % 2 == 0 and t < 8:
                first[t], first[t + 1] = gather(t), gather(t + 1)
            if 1 <= t < 9:
                second[t - 1] = fold(t - 1, *first.pop(t - 1))
            if t >= 2:
                store(t - 2, *second.pop(t - 2))
        send(p).start()
        return carry

    lax.fori_loop(0, 4, head_pair, 0)
    for p in range(4):
        send(p).wait()


def unpack_kernel(in_ref, dq_ref, dk_ref, dv_ref):
    out_refs = (dq_ref, dk_ref, dv_ref)
    left = iota((2, TILE, 8, 128), 3) < 64
    lane = iota((2 * DIM, 128), 1)
    row = iota((64, 256), 0)
    end_pick = ones_where(iota((64, 256), 1) == 24 * (row // 8) + 16 + row % 8)
    seconds, ends = [], []

    def gather(b):
        one, two = [
            in_ref[a].astype(F32).reshape(2, BACK // 8, 8, 128) for a in (2 * b, 2 * b + 1)
        ]
        first, second = one[:, :TILE], two[:, :TILE]
        third, fourth = one[:, TILE : 2 * TILE], two[:, TILE : 2 * TILE]
        seconds.extend([third.reshape(2 * DIM, 128), fourth.reshape(2 * DIM, 128)])
        ends.extend([one[:, 2 * TILE], two[:, 2 * TILE]])
        return (
            jnp.where(left, first, roll(second, 64)),
            jnp.where(left, roll(first, 64), second),
            jnp.where(left, third, roll(fourth, 64)),
        )

    def store(b, grads):
        for ref, grad in zip(out_refs, grads):
            ref[:, 128 * b : 128 * b + 128] = grad.reshape(2 * DIM, 128).astype(BF16)

    def shift(c):
        return [turn(x, 24 * a - 64 - 24 * c) for a, x in enumerate(seconds)]

    def join(c, moved):
        for tile, owners in ((0, range(6)), (1, range(5, 8))):
            total = last[:, 128 * tile : 128 * tile + 128]
            for a in owners:
                at = lane - (24 * a - 128 * tile)
                mine = (at >= 0) & (at < (24, 24, 16)[c])
                total = jnp.where(mine, moved[a], total)
            start = BULK + 128 * tile
            part = total[:, : 128 - 64 * tile].astype(BF16)
            out_refs[c][:, start : start + 128 - 64 * tile] = part

    ready = gather(0)
    for b in range(4):
        following = gather(b + 1) if b < 3 else None
        store(b, ready)
        ready = following
    ends = jnp.stack(ends, axis=1).reshape(2, 64, 128).astype(BF16)
    last = [dot(ends[h], end_pick, TN)[:DIM] for h in range(2)]
    last = jnp.concatenate(last, axis=0)
    ready = shift(0)
    for c in range(3):
        following = shift(c + 1) if c < 2 else None
        join(c, ready)
        ready = following


def softmax_t(scores):
    top = jnp.max(scores, axis=0, keepdims=True)
    weights = jnp.exp2((scores - top) * EXP_SCALE)
    return weights * (1.0 / jnp.sum(weights, axis=0, keepdims=True))


def time_kernel(in_ref, out_ref, held, tails, grads, made, sem):
    row = iota((256, 256), 0)
    order = ones_where(iota((256, 256), 1) == 128 * ((row // 4) % 2) + 4 * (row // 8) + row % 4)
    unit = ones_where(iota((DIM, DIM), 0) == iota((DIM, DIM), 1))
    lane = iota((8, 128), 1)
    upper = iota((8, 128), 0) < 4

    def arriving(j):
        firsts, rests, last = [], [], []
        for p in range(2):
            start = pl.multiple_of((2 * j + p) * 2 * SEND, 16)
            x = in_ref[pl.ds(start, 2 * SEND), :].astype(F32).reshape(2, SEND // 8, 8, 128)
            sides, more = [], []
            for f in range(2):
                sides.append(jnp.concatenate([x[f, :16], x[f, TILE:]], axis=0).reshape(256, 128))
                m = x[f, 2 * TILE :]
                ends = [
                    jnp.where(
                        lane < 32,
                        roll(m[t], 32),
                        jnp.where(lane < 64, roll(m[t + 1], 64), roll(m[t + 2], 96)),
                    )
                    for t in (0, 3)
                ]
                more.append(jnp.concatenate([m, ends[0][None], ends[1][None], m], axis=0))
            wide = jnp.concatenate(sides, axis=1).astype(BF16)
            firsts.append(dot(order, wide, NT))
            rests.append(jnp.concatenate([y.reshape(128, 128) for y in more], axis=1))
            last.append(jnp.where(upper, x[0, SEND // 8 - 1], x[1, SEND // 8 - 1]))
        rest = jnp.concatenate(rests, axis=0).astype(BF16)
        return firsts, dot(order[: 8 * 4 * 6], rest, NT), last

    def keep(j, firsts, rest, last):
        for p in range(2):
            at = pl.ds(pl.multiple_of((2 * j + p) * 8, 8), 8)
            for c in range(4):
                start = 128 * (c // 2)
                half = firsts[p][128 * (c % 2) : 128 * (c % 2) + 128, start : start + DIM]
                held[c, 0:16, at, 0:DIM] = half.reshape(16, 8, DIM)
                half = rest[48 * c : 48 * c + 48, 128 * p : 128 * p + DIM]
                held[c, 16:UNITS, at, 0:DIM] = half.reshape(6, 8, DIM)
            tails[at, :] = last[p]

    ahead(0, FRAMES // 4, 8, arriving, keep)
    pick = ones_where(iota((32, 128), 1) == iota((32, 128), 0) + 96)
    dots = dot(pick, tails[...].astype(BF16), NT)
    same = iota((ROWS, ROWS), 0) % 4 == iota((ROWS, ROWS), 1) % 4

    def load(u):
        q, k, v, g = [held[c, u, :, 0:DIM].astype(BF16) for c in range(4)]
        return q, k, g, dot(k, q, NT), dot(v, g, NT)

    following = load(0)
    for u in range(UNITS):
        q, k, g, scores, grad_attend = following
        if u + 1 < UNITS:
            following = load(u + 1)
        attend = softmax_t(jnp.where(same, scores, -1e30))
        dscore = (attend * (grad_attend - dots[u : u + 1, :])).astype(BF16)
        grads[0, u, :, 0:DIM] = dot(dscore, k, TN) * SCALE
        grads[1, u, :, 0:DIM] = dot(dscore, q, NN) * SCALE
        grads[2, u, :, 0:DIM] = dot(attend.astype(BF16), g, NN)

    def swap(x):
        pairs = x.reshape(x.shape[0] // 2, 2, 8, 128)
        even, odd = pairs[:, 0], pairs[:, 1]
        first = jnp.where(upper, even, pltpu.roll(odd, 4, 1))
        second = jnp.where(upper, pltpu.roll(even, 4, 1), odd)
        return first, second

    def leaving(i):
        at = pl.ds(pl.multiple_of(i * 8, 8), 8)
        sets = (
            (grads[0, 0:16, at, :], grads[1, 0:16, at, :]),
            (
                grads[2, 0:16, at, :],
                grads[0, 16:UNITS, at, :],
                grads[1, 16:UNITS, at, :],
                grads[2, 16:20, at, :],
            ),
        )
        turned = []
        for parts in sets:
            rows = jnp.concatenate(swap(jnp.concatenate(parts, axis=0)), axis=0)
            rows = rows.reshape(256, 128)[:, :DIM].astype(BF16)
            turned.append(dot(unit, rows, NT))
        ends = swap(jnp.where(lane < DIM, grads[2, 20:22, at, :], 0.0))
        return turned, ends

    def place(i, turned, ends):
        pieces = []
        for f in range(2):
            pieces += [t[:, 128 * f : 128 * f + 128] for t in turned] + [ends[f][0]]
        start = pl.multiple_of(i * 2 * BACK, 16)
        made[pl.ds(start, 2 * BACK), :] = jnp.concatenate(pieces, axis=0).astype(BF16)

    def send(part):
        rows = pl.ds(part * FRAMES * BACK // 2, FRAMES * BACK // 2)
        return pltpu.make_async_copy(made.at[rows, :], out_ref.at[rows, :], sem.at[part])

    for part in range(2):
        ahead(part, FRAMES // 4, 16, leaving, place)
        send(part).start()
    for part in range(2):
        send(part).wait()


def ahead(part, count, block, make, use):
    def step(j, carry):
        base = part * count + j * block
        ready = make(base)
        for t in range(block):
            following = make(base + t + 1) if t + 1 < block else None
            use(base + t, *ready)
            ready = following
        return carry

    lax.fori_loop(0, count // block, step, 0)


def space_kernel(q_ref, k_ref, v_ref, o_ref, g_ref, dq_ref, dk_ref, dv_ref):
    q2, k2, v2, o2, g2 = [ref[...].astype(F32) for ref in (q_ref, k_ref, v_ref, o_ref, g_ref)]
    dots = jnp.sum((g2 * o2).reshape(2, DIM, TOKENS), axis=1)
    grads = ([], [], [])
    for h in range(2):
        part = slice(h * DIM, (h + 1) * DIM)
        q, k, v, g = [x[part].astype(BF16) for x in (q2, k2, v2, g2)]
        k_rows, v_rows = k2[part].T.astype(BF16), v2[part].T.astype(BF16)
        dq, dk, dv = [], None, None
        for start, size in ((0, 256), (256, 256), (512, 192)):
            cols = slice(start, start + size)
            attend = softmax_t(dot(k_rows, q[:, cols], NN))
            shifted = dot(v_rows, g[:, cols], NN) - dots[h : h + 1, cols]
            dscore = (attend * shifted).astype(BF16)
            dq.append(dot(k, dscore, NN))
            dk_part = dot(q[:, cols], dscore, NT)
            dv_part = dot(g[:, cols], attend.astype(BF16), NT)
            dk = dk_part if dk is None else dk + dk_part
            dv = dv_part if dv is None else dv + dv_part
        grads[0].append(jnp.concatenate(dq, axis=1) * SCALE)
        grads[1].append(dk * SCALE)
        grads[2].append(dv)
    for ref, halves in zip((dq_ref, dk_ref, dv_ref), grads):
        ref[...] = jnp.concatenate(halves, axis=0).astype(BF16)


def call(kernel, out_shapes, args, flops, vmem, **specs):
    moved = sum(a.size * 2 for a in args) + sum(math.prod(o) * 2 for o in out_shapes)
    return pl.pallas_call(
        kernel,
        out_shape=tuple(jax.ShapeDtypeStruct(o, BF16) for o in out_shapes),
        compiler_params=pltpu.CompilerParams(vmem_limit_bytes=vmem * 1024 * 1024),
        cost_estimate=pl.CostEstimate(flops=flops, bytes_accessed=moved, transcendentals=0),
        name=kernel.__name__,
        **specs,
    )(*args)


HEAD_PAIR = pl.BlockSpec((2 * DIM, TOKENS), lambda p: (p, 0))


def pack(q, k, v, g, o):
    (sent,) = call(
        pack_kernel,
        [(8, HEADS * SEND, 128)],
        (q, k, v, g, o),
        10**9,
        60,
        in_specs=[pl.BlockSpec(memory_space=pltpu.HBM)] * 5,
        out_specs=(pl.BlockSpec(memory_space=pltpu.HBM),),
        scratch_shapes=[
            pltpu.VMEM((5, 4, 2 * DIM, TOKENS), BF16),
            pltpu.VMEM((4, 8, 2 * SEND, 128), BF16),
            pltpu.VMEM((EXTRA, 1024), BF16),
            pltpu.SemaphoreType.DMA((5, 4)),
            pltpu.SemaphoreType.DMA((4,)),
        ],
    )
    return sent


def unpack(back):
    return call(
        unpack_kernel,
        [(WIDTH, TOKENS)] * 3,
        (back.reshape(8, HEADS * BACK, 128),),
        10**9,
        50,
        grid=(4,),
        in_specs=[pl.BlockSpec((8, 2 * BACK, 128), lambda p: (0, p, 0))],
        out_specs=(HEAD_PAIR,) * 3,
    )


def time_grads(got):
    return call(
        time_kernel,
        [(FRAMES * BACK, 128)],
        (got,),
        10**10,
        50,
        in_specs=[pl.BlockSpec(memory_space=pltpu.VMEM)],
        out_specs=(pl.BlockSpec(memory_space=pltpu.HBM),),
        scratch_shapes=[
            pltpu.VMEM((4, UNITS, ROWS, 128), F32),
            pltpu.VMEM((ROWS, 128), F32),
            pltpu.VMEM((3, UNITS, ROWS, 128), F32),
            pltpu.VMEM((FRAMES * BACK, 128), BF16),
            pltpu.SemaphoreType.DMA((2,)),
        ],
    )[0]


def space_grads(*args):
    return call(
        space_kernel,
        [(WIDTH, TOKENS)] * 3,
        args,
        4 * 10**10,
        60,
        grid=(4,),
        in_specs=[HEAD_PAIR] * 5,
        out_specs=(HEAD_PAIR,) * 3,
    )


def exchange(x, rows):
    x = x.reshape(FRAMES, rows, 128)
    x = lax.all_to_all(x, "seq", split_axis=0, concat_axis=0, tiled=True)
    return x.reshape(FRAMES * rows, 128)


def body(*args):
    sq, sk, sv, so, sg, tq, tk, tv, to, tg = [jnp.swapaxes(x[0], 0, 1) for x in args]
    got = exchange(pack(tq, tk, tv, tg, to), SEND)
    space = space_grads(sq, sk, sv, so, sg)
    time = unpack(exchange(time_grads(got), BACK))
    return tuple(jnp.swapaxes(x, 0, 1)[None] for x in (*space, *time))


def solution(mesh):
    spec = P(("dp", "seq"), None, None)
    return jax.shard_map(
        body, mesh=mesh, in_specs=(spec,) * 10, out_specs=(spec,) * 6, check_vma=False
    )
```

time: 179 us -> 177 us (0.989)
  Pallas kernels: 42.7 us -> 40.6 us
    pallas_call x4, Pallas kernels: 42.7 us -> 40.6 us  [call(): pl.pallas_call(kernel, out_shape=tuple((jax.ShapeDtypeStruct(o, BF16) for...]
where the time goes in v2:
time: 177 us; the launch traced here: 176 us
  blocking collectives  88.8 us (50%)
  Pallas kernels  40.6 us (23%)
  waiting for transfers between devices  37.8 us (21%)
  starting transfers between devices  6.87 us (4%)
    all_to_all x1, blocking collectives, exchange(): x = lax.all_to_all(x, 'seq', split_axis=0, concat_axis=0, tiled=True)  88.8 us
    pallas_call x4, Pallas kernels, call(): pl.pallas_call(kernel, out_shape=tuple((jax.ShapeDtypeStruct(o, BF16) for...  40.6 us
    all_to_all x1, waiting for transfers between devices, exchange(): x = lax.all_to_all(x, 'seq', split_axis=0, concat_axis=0, tiled=True)  37.8 us
    all_to_all x1, starting transfers between devices, exchange(): x = lax.all_to_all(x, 'seq', split_axis=0, concat_axis=0, tiled=True)  6.87 us
  transfers between devices with their start and end apart: 1, of which 1 were waited for; matrix products, arithmetic and copies ran while one was open for 0% of the time, Pallas kernels for 11%

profile of v2, /device:TPU:2, one launch (start us, length us, event | category | flops | bytes accessed | tf_op | source)
XLA Modules:
  0.0 176.2 jit_solution(18177545024086439063)
XLA Ops:
  0.6 5.3 %pack_kernel.1 = bf16[8,1600,128]{2,1,0:T(8,128)(2,1)} custom-call(bf16[576,704]{1,0:T(8,128)(2,1)} %bitcast.56, bf16[576,704]{1,0:T(8,128)(2,1)} %bitcast.57, bf16[576,704]{1,0:T(8,128)(2,1)} %bitcast.58, bf16[576,704]{1,0:T(8,128)(2,1)} %bitcast.59, bf16[576,704]{1,0:T(8,128)(2,1)} %bitcast.60), custom_call_target="tpu_custom_call" | custom-call | flops 1000000000 | bytes 7331840 | tf_op jit(solution)/shard_map/pack_kernel/pallas_call | solution.py:349
  5.9 88.8 %all_to_all.10 = bf16[64,200,128]{2,1,0:T(8,128)(2,1)} all-to-all(bf16[64,200,128]{2,1,0:T(8,128)(2,1)} %bitcast.54), channel_id=1, replica_groups=mesh['dp'=4,'seq'=64] {'seq'}, dimensions={0} | all-to-all | bytes 6553600 | tf_op jit(solution)/shard_map/all_to_all | solution.py:429
  94.7 12.1 %time_kernel.1 = bf16[9728,128]{1,0:T(8,128)(2,1)S(1)} custom-call(bf16[12800,128]{1,0:T(8,128)(2,1)} %bitcast.55), custom_call_target="tpu_custom_call" | custom-call | flops 10000000000 | bytes 5767168 | tf_op jit(solution)/shard_map/time_kernel/pallas_call | solution.py:349
  106.8 0.0 copy-start
  106.8 1.5 copy-done
  108.3 6.9 %all-to-all-start.1 = ((bf16[64,152,128]{2,1,0:T(8,128)(2,1)}), bf16[64,152,128]{2,1,0:T(8,128)(2,1)S(1)}, u32[]{:S(2)}, u32[]{:S(2)}) async-start(bf16[64,152,128]{2,1,0:T(8,128)(2,1)} %bitcast.53), calls=%async_computation.1 | async-start | bytes 4980736 | tf_op jit(solution)/shard_map/all_to_all | solution.py:429
  115.1 20.1 %space_kernel.1 = (bf16[576,704]{1,0:T(8,128)(2,1)}, bf16[576,704]{1,0:T(8,128)(2,1)}, bf16[576,704]{1,0:T(8,128)(2,1)}) custom-call(bf16[576,704]{1,0:T(8,128)(2,1)} %bitcast.61, bf16[576,704]{1,0:T(8,128)(2,1)} %bitcast.62, bf16[576,704]{1,0:T(8,128)(2,1)} %bitcast.63, bf16[576,704]{1,0:T(8,128)(2,1)} %bitcast.64, bf16[576,704]{1,0:T(8,128)(2,1)} %bitcast.65), custom_call_target="tpu_custom_call" | custom-call | flops 40000000000 | bytes 6488064 | tf_op jit(solution)/shard_map/space_kernel/pallas_call | solution.py:349
  135.3 37.8 %all-to-all-done.1 = bf16[64,152,128]{2,1,0:T(8,128)(2,1)S(1)} async-done(((bf16[64,152,128]{2,1,0:T(8,128)(2,1)}), bf16[64,152,128]{2,1,0:T(8,128)(2,1)S(1)}, u32[]{:S(2)}, u32[]{:S(2)}) %all-to-all-start.1) | async-done | bytes 2490400 | tf_op jit(solution)/shard_map/all_to_all | solution.py:429
  173.1 3.1 %unpack_kernel.1 = (bf16[576,704]{1,0:T(8,128)(2,1)}, bf16[576,704]{1,0:T(8,128)(2,1)}, bf16[576,704]{1,0:T(8,128)(2,1)}) custom-call(bf16[8,1216,128]{2,1,0:T(8,128)(2,1)S(1)} %bitcast.52), custom_call_target="tpu_custom_call" | custom-call | flops 1000000000 | bytes 4923392 | tf_op jit(solution)/shard_map/unpack_kernel/pallas_call | solution.py:349
Async XLA Ops:
  106.8 1.5 copy-start
  108.3 64.8 %all-to-all-start.1 = ((bf16[64,152,128]{2,1,0:T(8,128)(2,1)}), bf16[64,152,128]{2,1,0:T(8,128)(2,1)S(1)}, u32[]{:S(2)}, u32[]{:S(2)}) async-start(bf16[64,152,128]{2,1,0:T(8,128)(2,1)} %bitcast.53), calls=%async_computation.1 | async-start | bytes 4980736 | tf_op jit(solution)/shard_map/all_to_all | solution.py:429

commit v3 on v2

--- a/solution.py
+++ b/solution.py
@@ -48,7 +48,7 @@
     return roll(x, shift % 128) if shift % 128 else x
 
 
-def pack_kernel(q_ref, k_ref, v_ref, g_ref, o_ref, out_ref, held, made, dot_pick, in_sem, out_sem):
+def pack_kernel(q_ref, k_ref, v_ref, g_ref, o_ref, out_ref, held, made, picks, dot_pick, in_sem, out_sem):
     refs = (q_ref, k_ref, v_ref, g_ref, o_ref)
 
     def fetch(c, p):
@@ -66,8 +66,11 @@
     row, lane = iota((EXTRA, 128), 0), iota((EXTRA, 128), 1)
     for a in range(8):
         at = row - 24 * a
-        mine = (at >= 0) & (at < 24) & (lane == 112 + at // 4)
-        dot_pick[:, 128 * a : 128 * a + 128] = ones_where(mine)
+        mine = (at >= 0) & (at < 24)
+        cols = slice(128 * a, 128 * a + 128)
+        dot_pick[:, cols] = ones_where(mine & (lane == 112 + at // 4))
+        for i, c in enumerate((2, 3)):
+            picks[i, :, cols] = ones_where(mine & (lane == at + 24 * c))
     token, lane = iota((128, 256), 0), iota((128, 256), 1)
     pick = (token // 64 == lane // 128) & ((token % 64) // 4 == lane % 128 - 96)
     pick = ones_where(pick)
@@ -85,6 +88,10 @@
         stacked = jnp.concatenate([kept[:, 128 * b : 128 * b + 128] for b in range(4)], axis=0)
         tail = dot(stacked, pick, NN)
         tail_more = dot(kept[:, BULK:], dot_pick[...], NN)
+        spread = None
+        for i, c in enumerate((2, 3)):
+            part = dot(held[c, p, :, BULK:], picks[i], NN)
+            spread = part if spread is None else spread + part
         fourth = [x[:, BULK : BULK + 128] for x in full]
         blank = jnp.zeros((2 * DIM, 64), F32)
         fifth = [jnp.concatenate([x[:, BULK + 128 :], blank], axis=1) for x in full]
@@ -102,10 +109,11 @@
                     joined = jnp.where(lane < 64, x, roll(y, 64))
                 pairs.append(joined.reshape(2, TILE, 8, 128))
             source = fourth if a < 5 else across if a == 5 else fifth
-            moved = [turn(x, 24 * c - 24 * a) for c, x in enumerate(source)]
-            rest = moved[3]
-            for c in (2, 1, 0):
-                rest = jnp.where(lane < 24 * c + 24, moved[c], rest)
+            rest = spread[:, 128 * a : 128 * a + 128]
+            for c in range(4):
+                if c not in (2, 3):
+                    at = lane - 24 * c
+                    rest = jnp.where((at >= 0) & (at < 24), turn(source[c], 24 * c - 24 * a), rest)
             return pairs, rest.reshape(2, TILE, 8, 128)
 
         def fold(a, pairs, rest):
@@ -137,59 +145,73 @@
         send(p).wait()
 
 
-def unpack_kernel(in_ref, dq_ref, dk_ref, dv_ref):
+def unpack_kernel(in_ref, dq_ref, dk_ref, dv_ref, made, sem):
     out_refs = (dq_ref, dk_ref, dv_ref)
     left = iota((2, TILE, 8, 128), 3) < 64
     lane = iota((2 * DIM, 128), 1)
     row = iota((64, 256), 0)
     end_pick = ones_where(iota((64, 256), 1) == 24 * (row // 8) + 16 + row % 8)
-    seconds, ends = [], []
-
-    def gather(b):
-        one, two = [
-            in_ref[a].astype(F32).reshape(2, BACK // 8, 8, 128) for a in (2 * b, 2 * b + 1)
-        ]
-        first, second = one[:, :TILE], two[:, :TILE]
-        third, fourth = one[:, TILE : 2 * TILE], two[:, TILE : 2 * TILE]
-        seconds.extend([third.reshape(2 * DIM, 128), fourth.reshape(2 * DIM, 128)])
-        ends.extend([one[:, 2 * TILE], two[:, 2 * TILE]])
-        return (
-            jnp.where(left, first, roll(second, 64)),
-            jnp.where(left, roll(first, 64), second),
-            jnp.where(left, third, roll(fourth, 64)),
-        )
-
-    def store(b, grads):
-        for ref, grad in zip(out_refs, grads):
-            ref[:, 128 * b : 128 * b + 128] = grad.reshape(2 * DIM, 128).astype(BF16)
-
-    def shift(c):
-        return [turn(x, 24 * a - 64 - 24 * c) for a, x in enumerate(seconds)]
-
-    def join(c, moved):
-        for tile, owners in ((0, range(6)), (1, range(5, 8))):
-            total = last[:, 128 * tile : 128 * tile + 128]
-            for a in owners:
-                at = lane - (24 * a - 128 * tile)
-                mine = (at >= 0) & (at < (24, 24, 16)[c])
-                total = jnp.where(mine, moved[a], total)
-            start = BULK + 128 * tile
-            part = total[:, : 128 - 64 * tile].astype(BF16)
-            out_refs[c][:, start : start + 128 - 64 * tile] = part
-
-    ready = gather(0)
-    for b in range(4):
-        following = gather(b + 1) if b < 3 else None
-        store(b, ready)
-        ready = following
-    ends = jnp.stack(ends, axis=1).reshape(2, 64, 128).astype(BF16)
-    last = [dot(ends[h], end_pick, TN)[:DIM] for h in range(2)]
-    last = jnp.concatenate(last, axis=0)
-    ready = shift(0)
-    for c in range(3):
-        following = shift(c + 1) if c < 2 else None
-        join(c, ready)
-        ready = following
+
+    def send(c, p):
+        rows = pl.ds(pl.multiple_of(p * 2 * DIM, 16), 2 * DIM)
+        return pltpu.make_async_copy(made.at[c, p], out_refs[c].at[rows, :], sem.at[c, p])
+
+    def head_pair(p, carry):
+        seconds, ends = [], []
+
+        def gather(b):
+            one, two = [
+                in_ref[a, pl.ds(pl.multiple_of(p * 2 * BACK, 16), 2 * BACK), :].astype(F32).reshape(2, BACK // 8, 8, 128) for a in (2 * b, 2 * b + 1)
+            ]
+            first, second = one[:, :TILE], two[:, :TILE]
+            third, fourth = one[:, TILE : 2 * TILE], two[:, TILE : 2 * TILE]
+            seconds.extend([third.reshape(2 * DIM, 128), fourth.reshape(2 * DIM, 128)])
+            ends.extend([one[:, 2 * TILE], two[:, 2 * TILE]])
+            return (
+                jnp.where(left, first, roll(second, 64)),
+                jnp.where(left, roll(first, 64), second),
+                jnp.where(left, third, roll(fourth, 64)),
+            )
+
+        def store(b, grads):
+            for c, grad in enumerate(grads):
+                made[c, p, :, 128 * b : 128 * b + 128] = grad.reshape(2 * DIM, 128).astype(BF16)
+
+        def shift(c):
+            return [turn(x, 24 * a - 64 - 24 * c) for a, x in enumerate(seconds)]
+
+        def join(c, moved):
+            for tile, owners in ((0, range(6)), (1, range(5, 8))):
+                total = last[:, 128 * tile : 128 * tile + 128]
+                for a in owners:
+                    at = lane - (24 * a - 128 * tile)
+                    mine = (at >= 0) & (at < (24, 24, 16)[c])
+                    total = jnp.where(mine, moved[a], total)
+                start = BULK + 128 * tile
+                part = total[:, : 128 - 64 * tile].astype(BF16)
+                made[c, p, :, start : start + 128 - 64 * tile] = part
+
+        ready = gather(0)
+        for b in range(4):
+            following = gather(b + 1) if b < 3 else None
+            store(b, ready)
+            ready = following
+        ends = jnp.stack(ends, axis=1).reshape(2, 64, 128).astype(BF16)
+        last = [dot(ends[h], end_pick, TN)[:DIM] for h in range(2)]
+        last = jnp.concatenate(last, axis=0)
+        ready = shift(0)
+        for c in range(3):
+            following = shift(c + 1) if c < 2 else None
+            join(c, ready)
+            ready = following
+        for c in range(3):
+            send(c, p).start()
+        return carry
+
+    lax.fori_loop(0, 4, head_pair, 0)
+    for p in range(4):
+        for c in range(3):
+            send(c, p).wait()
 
 
 def softmax_t(scores):
@@ -198,7 +220,14 @@
     return weights * (1.0 / jnp.sum(weights, axis=0, keepdims=True))
 
 
-def time_kernel(in_ref, out_ref, held, tails, grads, made, sem):
+def time_kernel(in_ref, out_ref, came, held, tails, grads, made, in_sem, out_sem):
+    def fetch(part):
+        rows = pl.ds(part * FRAMES * SEND // 4, FRAMES * SEND // 4)
+        return pltpu.make_async_copy(in_ref.at[rows, :], came.at[rows, :], in_sem.at[part])
+
+    for part in range(4):
+        fetch(part).start()
+
     row = iota((256, 256), 0)
     order = ones_where(iota((256, 256), 1) == 128 * ((row // 4) % 2) + 4 * (row // 8) + row % 4)
     unit = ones_where(iota((DIM, DIM), 0) == iota((DIM, DIM), 1))
@@ -209,7 +238,7 @@
         firsts, rests, last = [], [], []
         for p in range(2):
             start = pl.multiple_of((2 * j + p) * 2 * SEND, 16)
-            x = in_ref[pl.ds(start, 2 * SEND), :].astype(F32).reshape(2, SEND // 8, 8, 128)
+            x = came[pl.ds(start, 2 * SEND), :].astype(F32).reshape(2, SEND // 8, 8, 128)
             sides, more = [], []
             for f in range(2):
                 sides.append(jnp.concatenate([x[f, :16], x[f, TILE:]], axis=0).reshape(256, 128))
@@ -241,7 +270,9 @@
                 held[c, 16:UNITS, at, 0:DIM] = half.reshape(6, 8, DIM)
             tails[at, :] = last[p]
 
-    ahead(0, FRAMES // 4, 8, arriving, keep)
+    for part in range(4):
+        fetch(part).wait()
+        ahead(part, FRAMES // 16, 4, arriving, keep)
     pick = ones_where(iota((32, 128), 1) == iota((32, 128), 0) + 96)
     dots = dot(pick, tails[...].astype(BF16), NT)
     same = iota((ROWS, ROWS), 0) % 4 == iota((ROWS, ROWS), 1) % 4
@@ -250,16 +281,24 @@
         q, k, v, g = [held[c, u, :, 0:DIM].astype(BF16) for c in range(4)]
         return q, k, g, dot(k, q, NT), dot(v, g, NT)
 
-    following = load(0)
-    for u in range(UNITS):
-        q, k, g, scores, grad_attend = following
-        if u + 1 < UNITS:
-            following = load(u + 1)
+    def middle(u, q, k, g, scores, grad_attend):
         attend = softmax_t(jnp.where(same, scores, -1e30))
         dscore = (attend * (grad_attend - dots[u : u + 1, :])).astype(BF16)
+        return q, k, g, attend.astype(BF16), dscore
+
+    def finish(u, q, k, g, attend, dscore):
         grads[0, u, :, 0:DIM] = dot(dscore, k, TN) * SCALE
         grads[1, u, :, 0:DIM] = dot(dscore, q, NN) * SCALE
-        grads[2, u, :, 0:DIM] = dot(attend.astype(BF16), g, NN)
+        grads[2, u, :, 0:DIM] = dot(attend, g, NN)
+
+    loaded, ready = load(0), None
+    for u in range(UNITS + 1):
+        following = load(u + 1) if u + 1 < UNITS else None
+        if u > 0:
+            finish(u - 1, *ready)
+        if u < UNITS:
+            ready = middle(u, *loaded)
+        loaded = following
 
     def swap(x):
         pairs = x.reshape(x.shape[0] // 2, 2, 8, 128)
@@ -295,13 +334,13 @@
         made[pl.ds(start, 2 * BACK), :] = jnp.concatenate(pieces, axis=0).astype(BF16)
 
     def send(part):
-        rows = pl.ds(part * FRAMES * BACK // 2, FRAMES * BACK // 2)
-        return pltpu.make_async_copy(made.at[rows, :], out_ref.at[rows, :], sem.at[part])
-
-    for part in range(2):
-        ahead(part, FRAMES // 4, 16, leaving, place)
+        rows = pl.ds(part * FRAMES * BACK // 4, FRAMES * BACK // 4)
+        return pltpu.make_async_copy(made.at[rows, :], out_ref.at[rows, :], out_sem.at[part])
+
+    for part in range(4):
+        ahead(part, FRAMES // 8, 8, leaving, place)
         send(part).start()
-    for part in range(2):
+    for part in range(4):
         send(part).wait()
 
 
@@ -371,6 +410,7 @@
         scratch_shapes=[
             pltpu.VMEM((5, 4, 2 * DIM, TOKENS), BF16),
             pltpu.VMEM((4, 8, 2 * SEND, 128), BF16),
+            pltpu.VMEM((2, EXTRA, 1024), BF16),
             pltpu.VMEM((EXTRA, 1024), BF16),
             pltpu.SemaphoreType.DMA((5, 4)),
             pltpu.SemaphoreType.DMA((4,)),
@@ -386,9 +426,12 @@
         (back.reshape(8, HEADS * BACK, 128),),
         10**9,
         50,
-        grid=(4,),
-        in_specs=[pl.BlockSpec((8, 2 * BACK, 128), lambda p: (0, p, 0))],
-        out_specs=(HEAD_PAIR,) * 3,
+        in_specs=[pl.BlockSpec(memory_space=pltpu.VMEM)],
+        out_specs=(pl.BlockSpec(memory_space=pltpu.HBM),) * 3,
+        scratch_shapes=[
+            pltpu.VMEM((3, 4, 2 * DIM, TOKENS), BF16),
+            pltpu.SemaphoreType.DMA((3, 4)),
+        ],
     )
 
 
@@ -398,15 +441,17 @@
         [(FRAMES * BACK, 128)],
         (got,),
         10**10,
-        50,
-        in_specs=[pl.BlockSpec(memory_space=pltpu.VMEM)],
+        60,
+        in_specs=[pl.BlockSpec(memory_space=pltpu.HBM)],
         out_specs=(pl.BlockSpec(memory_space=pltpu.HBM),),
         scratch_shapes=[
+            pltpu.VMEM((FRAMES * SEND, 128), BF16),
             pltpu.VMEM((4, UNITS, ROWS, 128), F32),
             pltpu.VMEM((ROWS, 128), F32),
             pltpu.VMEM((3, UNITS, ROWS, 128), F32),
             pltpu.VMEM((FRAMES * BACK, 128), BF16),
-            pltpu.SemaphoreType.DMA((2,)),
+            pltpu.SemaphoreType.DMA((4,)),
+            pltpu.SemaphoreType.DMA((4,)),
         ],
     )[0]
 

time: 177 us -> 174 us (0.983)
  transfers between devices with their start and end apart: 1 -> 1, of which waited for: 1 -> 1; matrix products, arithmetic and copies ran while one was open for 0% -> 0% of each run, Pallas kernels for 11% -> 12%
where the time goes in v3:
time: 174 us; the launch traced here: 173 us
  blocking collectives  88.8 us (51%)
  Pallas kernels  39.1 us (22%)
  waiting for transfers between devices  37.8 us (22%)
  starting transfers between devices  6.87 us (4%)
    all_to_all x1, blocking collectives, exchange(): x = lax.all_to_all(x, 'seq', split_axis=0, concat_axis=0, tiled=True)  88.8 us
    pallas_call x4, Pallas kernels, call(): pl.pallas_call(kernel, out_shape=tuple((jax.ShapeDtypeStruct(o, BF16) for...  39.1 us
    all_to_all x1, waiting for transfers between devices, exchange(): x = lax.all_to_all(x, 'seq', split_axis=0, concat_axis=0, tiled=True)  37.8 us
    all_to_all x1, starting transfers between devices, exchange(): x = lax.all_to_all(x, 'seq', split_axis=0, concat_axis=0, tiled=True)  6.87 us
  transfers between devices with their start and end apart: 1, of which 1 were waited for; matrix products, arithmetic and copies ran while one was open for 0% of the time, Pallas kernels for 12%

profile of v3, /device:TPU:2, one launch (start us, length us, event | category | flops | bytes accessed | tf_op | source)
XLA Modules:
  0.0 173.4 jit_solution(9708702161904947790)
XLA Ops:
  0.6 4.6 %pack_kernel.1 = bf16[8,1600,128]{2,1,0:T(8,128)(2,1)} custom-call(bf16[576,704]{1,0:T(8,128)(2,1)} %bitcast.56, bf16[576,704]{1,0:T(8,128)(2,1)} %bitcast.57, bf16[576,704]{1,0:T(8,128)(2,1)} %bitcast.58, bf16[576,704]{1,0:T(8,128)(2,1)} %bitcast.59, bf16[576,704]{1,0:T(8,128)(2,1)} %bitcast.60), custom_call_target="tpu_custom_call" | custom-call | flops 1000000000 | bytes 7331840 | tf_op jit(solution)/shard_map/pack_kernel/pallas_call | solution.py:388
  5.3 88.8 %all_to_all.10 = bf16[64,200,128]{2,1,0:T(8,128)(2,1)} all-to-all(bf16[64,200,128]{2,1,0:T(8,128)(2,1)} %bitcast.53), channel_id=1, replica_groups=mesh['dp'=4,'seq'=64] {'seq'}, dimensions={0} | all-to-all | bytes 6553600 | tf_op jit(solution)/shard_map/all_to_all | solution.py:474
  94.1 11.4 %time_kernel.1 = bf16[9728,128]{1,0:T(8,128)(2,1)} custom-call(bf16[12800,128]{1,0:T(8,128)(2,1)} %bitcast.54), custom_call_target="tpu_custom_call" | custom-call | flops 10000000000 | bytes 5767168 | tf_op jit(solution)/shard_map/time_kernel/pallas_call | solution.py:388
  105.5 6.9 %all-to-all-start.1 = ((bf16[64,152,128]{2,1,0:T(8,128)(2,1)}), bf16[64,152,128]{2,1,0:T(8,128)(2,1)S(1)}, u32[]{:S(2)}, u32[]{:S(2)}) async-start(bf16[64,152,128]{2,1,0:T(8,128)(2,1)} %bitcast.55), calls=%async_computation.1 | async-start | bytes 4980736 | tf_op jit(solution)/shard_map/all_to_all | solution.py:474
  112.4 20.1 %space_kernel.1 = (bf16[576,704]{1,0:T(8,128)(2,1)}, bf16[576,704]{1,0:T(8,128)(2,1)}, bf16[576,704]{1,0:T(8,128)(2,1)}) custom-call(bf16[576,704]{1,0:T(8,128)(2,1)} %bitcast.61, bf16[576,704]{1,0:T(8,128)(2,1)} %bitcast.62, bf16[576,704]{1,0:T(8,128)(2,1)} %bitcast.63, bf16[576,704]{1,0:T(8,128)(2,1)} %bitcast.64, bf16[576,704]{1,0:T(8,128)(2,1)} %bitcast.65), custom_call_target="tpu_custom_call" | custom-call | flops 40000000000 | bytes 6488064 | tf_op jit(solution)/shard_map/space_kernel/pallas_call | solution.py:388
  132.5 37.8 %all-to-all-done.1 = bf16[64,152,128]{2,1,0:T(8,128)(2,1)S(1)} async-done(((bf16[64,152,128]{2,1,0:T(8,128)(2,1)}), bf16[64,152,128]{2,1,0:T(8,128)(2,1)S(1)}, u32[]{:S(2)}, u32[]{:S(2)}) %all-to-all-start.1) | async-done | bytes 2490400 | tf_op jit(solution)/shard_map/all_to_all | solution.py:474
  170.3 2.9 %unpack_kernel.1 = (bf16[576,704]{1,0:T(8,128)(2,1)}, bf16[576,704]{1,0:T(8,128)(2,1)}, bf16[576,704]{1,0:T(8,128)(2,1)}) custom-call(bf16[8,1216,128]{2,1,0:T(8,128)(2,1)S(1)} %bitcast.52), custom_call_target="tpu_custom_call" | custom-call | flops 1000000000 | bytes 4923392 | tf_op jit(solution)/shard_map/unpack_kernel/pallas_call | solution.py:388
Async XLA Ops:
  105.5 64.8 %all-to-all-start.1 = ((bf16[64,152,128]{2,1,0:T(8,128)(2,1)}), bf16[64,152,128]{2,1,0:T(8,128)(2,1)S(1)}, u32[]{:S(2)}, u32[]{:S(2)}) async-start(bf16[64,152,128]{2,1,0:T(8,128)(2,1)} %bitcast.55), calls=%async_computation.1 | async-start | bytes 4980736 | tf_op jit(solution)/shard_map/all_to_all | solution.py:474

commit v4 on v3

--- a/solution.py
+++ b/solution.py
@@ -167,9 +167,10 @@
             third, fourth = one[:, TILE : 2 * TILE], two[:, TILE : 2 * TILE]
             seconds.extend([third.reshape(2 * DIM, 128), fourth.reshape(2 * DIM, 128)])
             ends.extend([one[:, 2 * TILE], two[:, 2 * TILE]])
+            mixed = roll(jnp.where(left, second, first), 64)
             return (
-                jnp.where(left, first, roll(second, 64)),
-                jnp.where(left, roll(first, 64), second),
+                jnp.where(left, first, mixed),
+                jnp.where(left, mixed, second),
                 jnp.where(left, third, roll(fourth, 64)),
             )
 
@@ -194,21 +195,21 @@
         ready = gather(0)
         for b in range(4):
             following = gather(b + 1) if b < 3 else None
+            if b == 3:
+                moved = shift(0)
             store(b, ready)
             ready = following
         ends = jnp.stack(ends, axis=1).reshape(2, 64, 128).astype(BF16)
         last = [dot(ends[h], end_pick, TN)[:DIM] for h in range(2)]
         last = jnp.concatenate(last, axis=0)
-        ready = shift(0)
         for c in range(3):
             following = shift(c + 1) if c < 2 else None
-            join(c, ready)
-            ready = following
-        for c in range(3):
+            join(c, moved)
             send(c, p).start()
+            moved = following
         return carry
 
-    lax.fori_loop(0, 4, head_pair, 0)
+    lax.fori_loop(0, 4, head_pair, 0, unroll=True)
     for p in range(4):
         for c in range(3):
             send(c, p).wait()
@@ -253,32 +254,36 @@
                 ]
                 more.append(jnp.concatenate([m, ends[0][None], ends[1][None], m], axis=0))
             wide = jnp.concatenate(sides, axis=1).astype(BF16)
-            firsts.append(dot(order, wide, NT))
+            firsts.append(wide)
             rests.append(jnp.concatenate([y.reshape(128, 128) for y in more], axis=1))
             last.append(jnp.where(upper, x[0, SEND // 8 - 1], x[1, SEND // 8 - 1]))
         rest = jnp.concatenate(rests, axis=0).astype(BF16)
-        return firsts, dot(order[: 8 * 4 * 6], rest, NT), last
+        return firsts, rest, last
+
+    def ordering(j, firsts, rest, last):
+        return [dot(order, x, NT) for x in firsts], dot(order[: 8 * 4 * 6], rest, NT), last
 
     def keep(j, firsts, rest, last):
-        for p in range(2):
-            at = pl.ds(pl.multiple_of((2 * j + p) * 8, 8), 8)
-            for c in range(4):
-                start = 128 * (c // 2)
-                half = firsts[p][128 * (c % 2) : 128 * (c % 2) + 128, start : start + DIM]
-                held[c, 0:16, at, 0:DIM] = half.reshape(16, 8, DIM)
-                half = rest[48 * c : 48 * c + 48, 128 * p : 128 * p + DIM]
-                held[c, 16:UNITS, at, 0:DIM] = half.reshape(6, 8, DIM)
-            tails[at, :] = last[p]
+        at = pl.ds(pl.multiple_of(j * 16, 16), 16)
+        for c in range(4):
+            start = 128 * (c // 2)
+            rows = slice(128 * (c % 2), 128 * (c % 2) + 128)
+            halves = [x[rows, start : start + DIM].reshape(16, 8, DIM) for x in firsts]
+            held[c, 0:16, at, 0:DIM] = jnp.concatenate(halves, axis=1).astype(BF16)
+            rows = slice(48 * c, 48 * c + 48)
+            halves = [rest[rows, x : x + DIM].reshape(6, 8, DIM) for x in (0, 128)]
+            held[c, 16:UNITS, at, 0:DIM] = jnp.concatenate(halves, axis=1).astype(BF16)
+        tails[at, :] = jnp.concatenate(last, axis=0)
 
     for part in range(4):
         fetch(part).wait()
-        ahead(part, FRAMES // 16, 4, arriving, keep)
+        ahead(part, FRAMES // 16, 4, arriving, ordering, keep)
     pick = ones_where(iota((32, 128), 1) == iota((32, 128), 0) + 96)
     dots = dot(pick, tails[...].astype(BF16), NT)
     same = iota((ROWS, ROWS), 0) % 4 == iota((ROWS, ROWS), 1) % 4
 
     def load(u):
-        q, k, v, g = [held[c, u, :, 0:DIM].astype(BF16) for c in range(4)]
+        q, k, v, g = [held[c, u, :, 0:DIM] for c in range(4)]
         return q, k, g, dot(k, q, NT), dot(v, g, NT)
 
     def middle(u, q, k, g, scores, grad_attend):
@@ -321,10 +326,12 @@
         turned = []
         for parts in sets:
             rows = jnp.concatenate(swap(jnp.concatenate(parts, axis=0)), axis=0)
-            rows = rows.reshape(256, 128)[:, :DIM].astype(BF16)
-            turned.append(dot(unit, rows, NT))
+            turned.append(rows.reshape(256, 128)[:, :DIM].astype(BF16))
         ends = swap(jnp.where(lane < DIM, grads[2, 20:22, at, :], 0.0))
         return turned, ends
+
+    def turning(i, rows, ends):
+        return [dot(unit, x, NT) for x in rows], ends
 
     def place(i, turned, ends):
         pieces = []
@@ -338,20 +345,23 @@
         return pltpu.make_async_copy(made.at[rows, :], out_ref.at[rows, :], out_sem.at[part])
 
     for part in range(4):
-        ahead(part, FRAMES // 8, 8, leaving, place)
+        ahead(part, FRAMES // 8, 8, leaving, turning, place)
         send(part).start()
     for part in range(4):
         send(part).wait()
 
 
-def ahead(part, count, block, make, use):
+def ahead(part, count, block, make, work, use):
     def step(j, carry):
         base = part * count + j * block
-        ready = make(base)
-        for t in range(block):
-            following = make(base + t + 1) if t + 1 < block else None
-            use(base + t, *ready)
-            ready = following
+        made, worked = {}, {}
+        for t in range(block + 2):
+            if t < block:
+                made[t] = make(base + t)
+            if 1 <= t <= block:
+                worked[t - 1] = work(base + t - 1, *made.pop(t - 1))
+            if t >= 2:
+                use(base + t - 2, *worked.pop(t - 2))
         return carry
 
     lax.fori_loop(0, count // block, step, 0)
@@ -446,7 +456,7 @@
         out_specs=(pl.BlockSpec(memory_space=pltpu.HBM),),
         scratch_shapes=[
             pltpu.VMEM((FRAMES * SEND, 128), BF16),
-            pltpu.VMEM((4, UNITS, ROWS, 128), F32),
+            pltpu.VMEM((4, UNITS, ROWS, 128), BF16),
             pltpu.VMEM((ROWS, 128), F32),
             pltpu.VMEM((3, UNITS, ROWS, 128), F32),
             pltpu.VMEM((FRAMES * BACK, 128), BF16),

time: 174 us -> 173 us (level)
  no operation moved by 1% of the time
where the time goes in v4:
time: 173 us
  blocking collectives  88.8 us (51%)
  Pallas kernels  38.4 us (22%)
  waiting for transfers between devices  37.8 us (22%)
  starting transfers between devices  6.88 us (4%)
    all_to_all x1, blocking collectives, exchange(): x = lax.all_to_all(x, 'seq', split_axis=0, concat_axis=0, tiled=True)  88.8 us
    pallas_call x4, Pallas kernels, call(): pl.pallas_call(kernel, out_shape=tuple((jax.ShapeDtypeStruct(o, BF16) for...  38.4 us
    all_to_all x1, waiting for transfers between devices, exchange(): x = lax.all_to_all(x, 'seq', split_axis=0, concat_axis=0, tiled=True)  37.8 us
    all_to_all x1, starting transfers between devices, exchange(): x = lax.all_to_all(x, 'seq', split_axis=0, concat_axis=0, tiled=True)  6.88 us
  transfers between devices with their start and end apart: 1, of which 1 were waited for; matrix products, arithmetic and copies ran while one was open for 0% of the time, Pallas kernels for 12%

profile of v4, /device:TPU:2, one launch (start us, length us, event | category | flops | bytes accessed | tf_op | source)
XLA Modules:
  0.0 172.7 jit_solution(15064053566049486469)
XLA Ops:
  0.6 4.6 %pack_kernel.1 = bf16[8,1600,128]{2,1,0:T(8,128)(2,1)} custom-call(bf16[576,704]{1,0:T(8,128)(2,1)} %bitcast.56, bf16[576,704]{1,0:T(8,128)(2,1)} %bitcast.57, bf16[576,704]{1,0:T(8,128)(2,1)} %bitcast.58, bf16[576,704]{1,0:T(8,128)(2,1)} %bitcast.59, bf16[576,704]{1,0:T(8,128)(2,1)} %bitcast.60), custom_call_target="tpu_custom_call" | custom-call | flops 1000000000 | bytes 7331840 | tf_op jit(solution)/shard_map/pack_kernel/pallas_call | solution.py:398
  5.3 88.8 %all_to_all.10 = bf16[64,200,128]{2,1,0:T(8,128)(2,1)} all-to-all(bf16[64,200,128]{2,1,0:T(8,128)(2,1)} %bitcast.53), channel_id=1, replica_groups=mesh['dp'=4,'seq'=64] {'seq'}, dimensions={0} | all-to-all | bytes 6553600 | tf_op jit(solution)/shard_map/all_to_all | solution.py:484
  94.1 11.2 %time_kernel.1 = bf16[9728,128]{1,0:T(8,128)(2,1)} custom-call(bf16[12800,128]{1,0:T(8,128)(2,1)} %bitcast.54), custom_call_target="tpu_custom_call" | custom-call | flops 10000000000 | bytes 5767168 | tf_op jit(solution)/shard_map/time_kernel/pallas_call | solution.py:398
  105.3 6.9 %all-to-all-start.1 = ((bf16[64,152,128]{2,1,0:T(8,128)(2,1)}), bf16[64,152,128]{2,1,0:T(8,128)(2,1)S(1)}, u32[]{:S(2)}, u32[]{:S(2)}) async-start(bf16[64,152,128]{2,1,0:T(8,128)(2,1)} %bitcast.55), calls=%async_computation.1 | async-start | bytes 4980736 | tf_op jit(solution)/shard_map/all_to_all | solution.py:484
  112.2 20.1 %space_kernel.1 = (bf16[576,704]{1,0:T(8,128)(2,1)}, bf16[576,704]{1,0:T(8,128)(2,1)}, bf16[576,704]{1,0:T(8,128)(2,1)}) custom-call(bf16[576,704]{1,0:T(8,128)(2,1)} %bitcast.61, bf16[576,704]{1,0:T(8,128)(2,1)} %bitcast.62, bf16[576,704]{1,0:T(8,128)(2,1)} %bitcast.63, bf16[576,704]{1,0:T(8,128)(2,1)} %bitcast.64, bf16[576,704]{1,0:T(8,128)(2,1)} %bitcast.65), custom_call_target="tpu_custom_call" | custom-call | flops 40000000000 | bytes 6488064 | tf_op jit(solution)/shard_map/space_kernel/pallas_call | solution.py:398
  132.4 37.8 %all-to-all-done.1 = bf16[64,152,128]{2,1,0:T(8,128)(2,1)S(1)} async-done(((bf16[64,152,128]{2,1,0:T(8,128)(2,1)}), bf16[64,152,128]{2,1,0:T(8,128)(2,1)S(1)}, u32[]{:S(2)}, u32[]{:S(2)}) %all-to-all-start.1) | async-done | bytes 2490400 | tf_op jit(solution)/shard_map/all_to_all | solution.py:484
  170.2 2.4 %unpack_kernel.1 = (bf16[576,704]{1,0:T(8,128)(2,1)}, bf16[576,704]{1,0:T(8,128)(2,1)}, bf16[576,704]{1,0:T(8,128)(2,1)}) custom-call(bf16[8,1216,128]{2,1,0:T(8,128)(2,1)S(1)} %bitcast.52), custom_call_target="tpu_custom_call" | custom-call | flops 1000000000 | bytes 4923392 | tf_op jit(solution)/shard_map/unpack_kernel/pallas_call | solution.py:398
Async XLA Ops:
  105.3 64.8 %all-to-all-start.1 = ((bf16[64,152,128]{2,1,0:T(8,128)(2,1)}), bf16[64,152,128]{2,1,0:T(8,128)(2,1)S(1)}, u32[]{:S(2)}, u32[]{:S(2)}) async-start(bf16[64,152,128]{2,1,0:T(8,128)(2,1)} %bitcast.55), calls=%async_computation.1 | async-start | bytes 4980736 | tf_op jit(solution)/shard_map/all_to_all | solution.py:484

commit v5 on v4

--- a/solution.py
+++ b/solution.py
@@ -5,6 +5,7 @@
 from jax import lax
 from jax.experimental import pallas as pl
 from jax.experimental.pallas import tpu as pltpu
+from jax.sharding import Mesh
 from jax.sharding import PartitionSpec as P
 
 HEADS = 8
@@ -21,6 +22,7 @@
 TILE = DIM // 8
 SCALE = 1.0 / math.sqrt(DIM)
 EXP_SCALE = SCALE * math.log2(math.e)
+PEERS = ("x", "z", "y")
 BF16 = jnp.bfloat16
 F32 = jnp.float32
 NN = ((1,), (0,))
@@ -481,7 +483,7 @@
 
 def exchange(x, rows):
     x = x.reshape(FRAMES, rows, 128)
-    x = lax.all_to_all(x, "seq", split_axis=0, concat_axis=0, tiled=True)
+    x = lax.all_to_all(x, PEERS, split_axis=0, concat_axis=0, tiled=True)
     return x.reshape(FRAMES * rows, 128)
 
 
@@ -494,7 +496,8 @@
 
 
 def solution(mesh):
-    spec = P(("dp", "seq"), None, None)
+    fine = Mesh(mesh.devices.reshape(-1, 8, 2, 4), ("dp", "z", "y", "x"))
+    spec = P(("dp", "z", "y", "x"), None, None)
     return jax.shard_map(
-        body, mesh=mesh, in_specs=(spec,) * 10, out_specs=(spec,) * 6, check_vma=False
+        body, mesh=fine, in_specs=(spec,) * 10, out_specs=(spec,) * 6, check_vma=False
     )

time: 173 us -> 174 us (level)
  no operation moved by 1% of the time
where the time goes in v5:
time: 174 us; the launch traced here: 173 us
  blocking collectives  88.8 us (51%)
  Pallas kernels  38.4 us (22%)
  waiting for transfers between devices  38 us (22%)
  starting transfers between devices  6.98 us (4%)
    all_to_all x1, blocking collectives, exchange(): x = lax.all_to_all(x, PEERS, split_axis=0, concat_axis=0, tiled=True)  88.8 us
    pallas_call x4, Pallas kernels, call(): pl.pallas_call(kernel, out_shape=tuple((jax.ShapeDtypeStruct(o, BF16) for...  38.4 us
    all_to_all x1, waiting for transfers between devices, exchange(): x = lax.all_to_all(x, PEERS, split_axis=0, concat_axis=0, tiled=True)  38 us
    all_to_all x1, starting transfers between devices, exchange(): x = lax.all_to_all(x, PEERS, split_axis=0, concat_axis=0, tiled=True)  6.98 us
  transfers between devices with their start and end apart: 1, of which 1 were waited for; matrix products, arithmetic and copies ran while one was open for 0% of the time, Pallas kernels for 12%

profile of v5, /device:TPU:2, one launch (start us, length us, event | category | flops | bytes accessed | tf_op | source)
XLA Modules:
  0.0 173.0 jit_solution(14179062929047844694)
XLA Ops:
  0.6 4.6 %pack_kernel.1 = bf16[8,1600,128]{2,1,0:T(8,128)(2,1)} custom-call(bf16[576,704]{1,0:T(8,128)(2,1)} %bitcast.56, bf16[576,704]{1,0:T(8,128)(2,1)} %bitcast.57, bf16[576,704]{1,0:T(8,128)(2,1)} %bitcast.58, bf16[576,704]{1,0:T(8,128)(2,1)} %bitcast.59, bf16[576,704]{1,0:T(8,128)(2,1)} %bitcast.60), custom_call_target="tpu_custom_call" | custom-call | flops 1000000000 | bytes 7331840 | tf_op jit(solution)/shard_map/pack_kernel/pallas_call | solution.py:400
  5.3 88.8 %all_to_all.10 = bf16[64,200,128]{2,1,0:T(8,128)(2,1)} all-to-all(bf16[64,200,128]{2,1,0:T(8,128)(2,1)} %bitcast.53), channel_id=1, replica_groups=mesh['dp'=4,'z'=8,'y'=2,'x'=4] {'x','z','y'}, dimensions={0} | all-to-all | bytes 6553600 | tf_op jit(solution)/shard_map/all_to_all | solution.py:486
  94.1 11.3 %time_kernel.1 = bf16[9728,128]{1,0:T(8,128)(2,1)} custom-call(bf16[12800,128]{1,0:T(8,128)(2,1)} %bitcast.54), custom_call_target="tpu_custom_call" | custom-call | flops 10000000000 | bytes 5767168 | tf_op jit(solution)/shard_map/time_kernel/pallas_call | solution.py:400
  105.4 7.0 %all-to-all-start.1 = ((bf16[64,152,128]{2,1,0:T(8,128)(2,1)}), bf16[64,152,128]{2,1,0:T(8,128)(2,1)S(1)}, u32[]{:S(2)}, u32[]{:S(2)}) async-start(bf16[64,152,128]{2,1,0:T(8,128)(2,1)} %bitcast.55), calls=%async_computation.1 | async-start | bytes 4980736 | tf_op jit(solution)/shard_map/all_to_all | solution.py:486
  112.3 20.1 %space_kernel.1 = (bf16[576,704]{1,0:T(8,128)(2,1)}, bf16[576,704]{1,0:T(8,128)(2,1)}, bf16[576,704]{1,0:T(8,128)(2,1)}) custom-call(bf16[576,704]{1,0:T(8,128)(2,1)} %bitcast.61, bf16[576,704]{1,0:T(8,128)(2,1)} %bitcast.62, bf16[576,704]{1,0:T(8,128)(2,1)} %bitcast.63, bf16[576,704]{1,0:T(8,128)(2,1)} %bitcast.64, bf16[576,704]{1,0:T(8,128)(2,1)} %bitcast.65), custom_call_target="tpu_custom_call" | custom-call | flops 40000000000 | bytes 6488064 | tf_op jit(solution)/shard_map/space_kernel/pallas_call | solution.py:400
  132.5 38.0 %all-to-all-done.1 = bf16[64,152,128]{2,1,0:T(8,128)(2,1)S(1)} async-done(((bf16[64,152,128]{2,1,0:T(8,128)(2,1)}), bf16[64,152,128]{2,1,0:T(8,128)(2,1)S(1)}, u32[]{:S(2)}, u32[]{:S(2)}) %all-to-all-start.1) | async-done | bytes 2490400 | tf_op jit(solution)/shard_map/all_to_all | solution.py:486
  170.5 2.4 %unpack_kernel.1 = (bf16[576,704]{1,0:T(8,128)(2,1)}, bf16[576,704]{1,0:T(8,128)(2,1)}, bf16[576,704]{1,0:T(8,128)(2,1)}) custom-call(bf16[8,1216,128]{2,1,0:T(8,128)(2,1)S(1)} %bitcast.52), custom_call_target="tpu_custom_call" | custom-call | flops 1000000000 | bytes 4923392 | tf_op jit(solution)/shard_map/unpack_kernel/pallas_call | solution.py:400
Async XLA Ops:
  105.4 65.1 %all-to-all-start.1 = ((bf16[64,152,128]{2,1,0:T(8,128)(2,1)}), bf16[64,152,128]{2,1,0:T(8,128)(2,1)S(1)}, u32[]{:S(2)}, u32[]{:S(2)}) async-start(bf16[64,152,128]{2,1,0:T(8,128)(2,1)} %bitcast.55), calls=%async_computation.1 | async-start | bytes 4980736 | tf_op jit(solution)/shard_map/all_to_all | solution.py:486

commit v6 on v4

--- a/solution.py
+++ b/solution.py
@@ -221,14 +221,7 @@
     return weights * (1.0 / jnp.sum(weights, axis=0, keepdims=True))
 
 
-def time_kernel(in_ref, out_ref, came, held, tails, grads, made, in_sem, out_sem):
-    def fetch(part):
-        rows = pl.ds(part * FRAMES * SEND // 4, FRAMES * SEND // 4)
-        return pltpu.make_async_copy(in_ref.at[rows, :], came.at[rows, :], in_sem.at[part])
-
-    for part in range(4):
-        fetch(part).start()
-
+def time_kernel(in_ref, out_ref, held, tails, grads, made, out_sem):
     row = iota((256, 256), 0)
     order = ones_where(iota((256, 256), 1) == 128 * ((row // 4) % 2) + 4 * (row // 8) + row % 4)
     unit = ones_where(iota((DIM, DIM), 0) == iota((DIM, DIM), 1))
@@ -239,7 +232,7 @@
         firsts, rests, last = [], [], []
         for p in range(2):
             start = pl.multiple_of((2 * j + p) * 2 * SEND, 16)
-            x = came[pl.ds(start, 2 * SEND), :].astype(F32).reshape(2, SEND // 8, 8, 128)
+            x = in_ref[pl.ds(start, 2 * SEND), :].astype(F32).reshape(2, SEND // 8, 8, 128)
             sides, more = [], []
             for f in range(2):
                 sides.append(jnp.concatenate([x[f, :16], x[f, TILE:]], axis=0).reshape(256, 128))
@@ -275,9 +268,7 @@
             held[c, 16:UNITS, at, 0:DIM] = jnp.concatenate(halves, axis=1).astype(BF16)
         tails[at, :] = jnp.concatenate(last, axis=0)
 
-    for part in range(4):
-        fetch(part).wait()
-        ahead(part, FRAMES // 16, 4, arriving, ordering, keep)
+    ahead(0, FRAMES // 4, 8, arriving, ordering, keep)
     pick = ones_where(iota((32, 128), 1) == iota((32, 128), 0) + 96)
     dots = dot(pick, tails[...].astype(BF16), NT)
     same = iota((ROWS, ROWS), 0) % 4 == iota((ROWS, ROWS), 1) % 4
@@ -451,31 +442,36 @@
         [(FRAMES * BACK, 128)],
         (got,),
         10**10,
-        60,
-        in_specs=[pl.BlockSpec(memory_space=pltpu.HBM)],
+        48,
+        in_specs=[pl.BlockSpec(memory_space=pltpu.VMEM)],
         out_specs=(pl.BlockSpec(memory_space=pltpu.HBM),),
         scratch_shapes=[
-            pltpu.VMEM((FRAMES * SEND, 128), BF16),
             pltpu.VMEM((4, UNITS, ROWS, 128), BF16),
             pltpu.VMEM((ROWS, 128), F32),
             pltpu.VMEM((3, UNITS, ROWS, 128), F32),
             pltpu.VMEM((FRAMES * BACK, 128), BF16),
             pltpu.SemaphoreType.DMA((4,)),
-            pltpu.SemaphoreType.DMA((4,)),
         ],
     )[0]
 
 
-def space_grads(*args):
+def space_grads(half, args, before=()):
+    spec = pl.BlockSpec((2 * DIM, TOKENS), lambda p: (2 * half + p, 0))
+
+    def kernel(*refs):
+        space_kernel(*refs[:5], *refs[-3:])
+
+    kernel.__name__ = "space_kernel"
     return call(
-        space_kernel,
+        kernel,
         [(WIDTH, TOKENS)] * 3,
-        args,
-        4 * 10**10,
+        (*args, *before),
+        2 * 10**10,
         60,
-        grid=(4,),
-        in_specs=[HEAD_PAIR] * 5,
-        out_specs=(HEAD_PAIR,) * 3,
+        grid=(2,),
+        in_specs=[spec] * 5 + [pl.BlockSpec(memory_space=pl.ANY)] * len(before),
+        out_specs=(spec,) * 3,
+        input_output_aliases={5 + n: n for n in range(len(before))},
     )
 
 
@@ -488,8 +484,12 @@
 def body(*args):
     sq, sk, sv, so, sg, tq, tk, tv, to, tg = [jnp.swapaxes(x[0], 0, 1) for x in args]
     got = exchange(pack(tq, tk, tv, tg, to), SEND)
-    space = space_grads(sq, sk, sv, so, sg)
-    time = unpack(exchange(time_grads(got), BACK))
+    early = space_grads(0, (sq, sk, sv, so, sg))
+    got, early = lax.optimization_barrier((got, early))
+    done, early = lax.optimization_barrier((time_grads(got), early))
+    back = exchange(done, BACK)
+    space = space_grads(1, (sq, sk, sv, so, sg), early)
+    time = unpack(back)
     return tuple(jnp.swapaxes(x, 0, 1)[None] for x in (*space, *time))
 
 

time: 173 us -> 173 us (level)
  blocking collectives: 88.8 us -> 0 us
  waiting for transfers between devices: 37.8 us -> 111 us
  starting transfers between devices: 6.88 us -> 20.5 us
    all_to_all x1 -> x0, blocking collectives: 88.8 us -> none  [exchange(): x = lax.all_to_all(x, 'seq', split_axis=0, concat_axis=0, tiled=True)]
    all_to_all x1 -> x2, waiting for transfers between devices: 37.8 us -> 111 us  [exchange(): x = lax.all_to_all(x, 'seq', split_axis=0, concat_axis=0, tiled=True)]
    all_to_all x1 -> x2, starting transfers between devices: 6.88 us -> 20.5 us  [exchange(): x = lax.all_to_all(x, 'seq', split_axis=0, concat_axis=0, tiled=True)]
    pallas_call x4 -> x5, Pallas kernels: 38.4 us -> 39.6 us  [call(): pl.pallas_call(kernel, out_shape=tuple((jax.ShapeDtypeStruct(o, BF16) for...]
  transfers between devices with their start and end apart: 1 -> 2, of which waited for: 1 -> 2; matrix products, arithmetic and copies ran while one was open for 0% -> 0% of each run, Pallas kernels for 12% -> 13%
where the time goes in v6:
time: 173 us
  waiting for transfers between devices  111 us (64%)
  Pallas kernels  39.6 us (23%)
  starting transfers between devices  20.5 us (12%)
    all_to_all x2, waiting for transfers between devices, exchange(): x = lax.all_to_all(x, 'seq', split_axis=0, concat_axis=0, tiled=True)  111 us
    pallas_call x5, Pallas kernels, call(): pl.pallas_call(kernel, out_shape=tuple((jax.ShapeDtypeStruct(o, BF16) for...  39.6 us
    all_to_all x2, starting transfers between devices, exchange(): x = lax.all_to_all(x, 'seq', split_axis=0, concat_axis=0, tiled=True)  20.5 us
  transfers between devices with their start and end apart: 2, of which 2 were waited for; matrix products, arithmetic and copies ran while one was open for 0% of the time, Pallas kernels for 13%

profile of v6, /device:TPU:2, one launch (start us, length us, event | category | flops | bytes accessed | tf_op | source)
XLA Modules:
  0.0 173.0 jit_solution(4420541164791208471)
XLA Ops:
  0.6 4.6 %pack_kernel.1 = bf16[8,1600,128]{2,1,0:T(8,128)(2,1)} custom-call(bf16[576,704]{1,0:T(8,128)(2,1)} %bitcast.56, bf16[576,704]{1,0:T(8,128)(2,1)} %bitcast.57, bf16[576,704]{1,0:T(8,128)(2,1)} %bitcast.58, bf16[576,704]{1,0:T(8,128)(2,1)} %bitcast.59, bf16[576,704]{1,0:T(8,128)(2,1)} %bitcast.60), custom_call_target="tpu_custom_call" | custom-call | flops 1000000000 | bytes 7331840 | tf_op jit(solution)/shard_map/pack_kernel/pallas_call | solution.py:389
  5.3 13.0 %all-to-all-start = ((bf16[64,200,128]{2,1,0:T(8,128)(2,1)}), bf16[64,200,128]{2,1,0:T(8,128)(2,1)S(1)}, u32[]{:S(2)}, u32[]{:S(2)}) async-start(bf16[64,200,128]{2,1,0:T(8,128)(2,1)} %bitcast.55), calls=%async_computation | async-start | bytes 6553600 | tf_op jit(solution)/shard_map/all_to_all | solution.py:480
  18.3 11.1 %space_kernel.2 = (bf16[576,704]{1,0:T(8,128)(2,1)}, bf16[576,704]{1,0:T(8,128)(2,1)}, bf16[576,704]{1,0:T(8,128)(2,1)}) custom-call(bf16[576,704]{1,0:T(8,128)(2,1)} %bitcast.61, bf16[576,704]{1,0:T(8,128)(2,1)} %bitcast.63, bf16[576,704]{1,0:T(8,128)(2,1)} %bitcast.65, bf16[576,704]{1,0:T(8,128)(2,1)} %bitcast.67, bf16[576,704]{1,0:T(8,128)(2,1)} %bitcast.69), custom_call_target="tpu_custom_call" | custom-call | flops 20000000000 | bytes 6488064 | tf_op jit(solution)/shard_map/space_kernel/pallas_call | solution.py:389
  29.4 64.0 %all-to-all-done = bf16[64,200,128]{2,1,0:T(8,128)(2,1)S(1)} async-done(((bf16[64,200,128]{2,1,0:T(8,128)(2,1)}), bf16[64,200,128]{2,1,0:T(8,128)(2,1)S(1)}, u32[]{:S(2)}, u32[]{:S(2)}) %all-to-all-start) | async-done | bytes 3276832 | tf_op jit(solution)/shard_map/all_to_all | solution.py:480
  93.4 10.5 %time_kernel.1 = bf16[9728,128]{1,0:T(8,128)(2,1)S(1)} custom-call(bf16[12800,128]{1,0:T(8,128)(2,1)S(1)} %bitcast.52), custom_call_target="tpu_custom_call" | custom-call | flops 10000000000 | bytes 5767168 | tf_op jit(solution)/shard_map/time_kernel/pallas_call | solution.py:389
  103.9 0.0 copy-start
  103.9 1.5 copy-done
  105.4 7.5 %all-to-all-start.1 = ((bf16[64,152,128]{2,1,0:T(8,128)(2,1)}), bf16[64,152,128]{2,1,0:T(8,128)(2,1)S(1)}, u32[]{:S(2)}, u32[]{:S(2)}) async-start(bf16[64,152,128]{2,1,0:T(8,128)(2,1)} %bitcast.54), calls=%async_computation.1 | async-start | bytes 4980736 | tf_op jit(solution)/shard_map/all_to_all | solution.py:480
  112.8 11.1 %space_kernel.3 = (bf16[576,704]{1,0:T(8,128)(2,1)}, bf16[576,704]{1,0:T(8,128)(2,1)}, bf16[576,704]{1,0:T(8,128)(2,1)}) custom-call(bf16[576,704]{1,0:T(8,128)(2,1)} %bitcast.62, bf16[576,704]{1,0:T(8,128)(2,1)} %bitcast.64, bf16[576,704]{1,0:T(8,128)(2,1)} %bitcast.66, ...), custom_call_target="tpu_custom_call", output_to_operand_aliasing={{0}: (5, {}), {1}: (6, {}), {2}: (7, {})} | custom-call | flops 20000000000 | bytes 8921088 | tf_op jit(solution)/shard_map/space_kernel/pallas_call | solution.py:389
  123.9 46.6 %all-to-all-done.1 = bf16[64,152,128]{2,1,0:T(8,128)(2,1)S(1)} async-done(((bf16[64,152,128]{2,1,0:T(8,128)(2,1)}), bf16[64,152,128]{2,1,0:T(8,128)(2,1)S(1)}, u32[]{:S(2)}, u32[]{:S(2)}) %all-to-all-start.1) | async-done | bytes 2490400 | tf_op jit(solution)/shard_map/all_to_all | solution.py:480
  170.5 2.4 %unpack_kernel.1 = (bf16[576,704]{1,0:T(8,128)(2,1)}, bf16[576,704]{1,0:T(8,128)(2,1)}, bf16[576,704]{1,0:T(8,128)(2,1)}) custom-call(bf16[8,1216,128]{2,1,0:T(8,128)(2,1)S(1)} %bitcast.53), custom_call_target="tpu_custom_call" | custom-call | flops 1000000000 | bytes 4923392 | tf_op jit(solution)/shard_map/unpack_kernel/pallas_call | solution.py:389
Async XLA Ops:
  5.3 88.1 %all-to-all-start = ((bf16[64,200,128]{2,1,0:T(8,128)(2,1)}), bf16[64,200,128]{2,1,0:T(8,128)(2,1)S(1)}, u32[]{:S(2)}, u32[]{:S(2)}) async-start(bf16[64,200,128]{2,1,0:T(8,128)(2,1)} %bitcast.55), calls=%async_computation | async-start | bytes 6553600 | tf_op jit(solution)/shard_map/all_to_all | solution.py:480
  103.9 1.5 copy-start
  105.4 65.1 %all-to-all-start.1 = ((bf16[64,152,128]{2,1,0:T(8,128)(2,1)}), bf16[64,152,128]{2,1,0:T(8,128)(2,1)S(1)}, u32[]{:S(2)}, u32[]{:S(2)}) async-start(bf16[64,152,128]{2,1,0:T(8,128)(2,1)} %bitcast.54), calls=%async_computation.1 | async-start | bytes 4980736 | tf_op jit(solution)/shard_map/all_to_all | solution.py:480
